TPU v7x, 32 devices: a whole 2x2x4 slice. The times are simulated.
32 devices in a mesh: src: 8 (over z, y), seg: 4 (over x, core).
Axes of the slice: x: 2, y: 2, z: 4, core: 2. Of those that a mesh axis runs over, the one named last changes fastest.
Arguments:
- residual: float32 [524288], P(('src', 'seg')), may hold values from -24 to 24
- obs_weight: float32 [524288], P(('src', 'seg')), may hold values from 0.25 to 4
- time_frac: float32 [524288], P(('src', 'seg')), may hold values from 0 to 0.99
- src_partials: float32 [5, 524288], P(None, ('src', 'seg')), may hold values from -6 to 6
- att_dir: float32 [3, 524288], P(None, ('src', 'seg')), may hold values from -6 to 6
- src_prior: float32 [5, 16384], P(None, 'src'), may hold values from 4 to 40
- att_prior: float32 [3, 2048], P(None, ('src', 'seg')), may hold values from 16 to 128
- obs_source: int32 [524288], P(('src', 'seg')), may hold values from 0 to 2047, as said below
- obs_interval: int32 [524288], P(('src', 'seg')), may hold values from 0 to 2047, as said below
- obs_count: int32 [32, 8], P(('src', 'seg')), may hold values from 256 to 2048, as said below
Outputs:
- src_update: float32 [5, 16384], P(None, 'src')
- att_update: float32 [3, 2048], P(None, ('src', 'seg'))
- residual_out: float32 [524288], P(('src', 'seg'))
Inputs may be any that keep to these rules, and one draw needn't show every extreme that they name: obs_source of a slot on row r of obs_count (slot i with r = i // 16384) is the index of its source within the src block r // 4. A slot of row r in block b has an interval owned by knot block t = b * 4 + (r mod 4): obs_interval lies in t * 64 to (t + 1) * 64 - 1. `obs_count`: row r counts the live slots, from the start, of the 8 blocks of device r; for every seg index one block index is full (2048) on every row of that seg index.
All inputs are finite; a program needn't handle non-finite values.
Results may differ from a plain program's by a relative error of at most 0.0003.
Values sent between devices are 32-bit elements; how exact they have to be, the bound alone decides.
A program may use at most 128 MiB of HBM per device.

v0:
```python
import jax
import jax.numpy as jnp
from jax import lax
from jax.sharding import PartitionSpec as P

ITERS_ATT = 6


param_pairs = [
    (0, 0),
    (0, 1),
    (0, 2),
    (0, 3),
    (0, 4),
    (1, 1),
    (1, 2),
    (1, 3),
    (1, 4),
    (2, 2),
    (2, 3),
    (2, 4),
    (3, 3),
    (3, 4),
    (4, 4),
]
sym_pairs = [(0, 0), (0, 1), (0, 2), (1, 1), (1, 2), (2, 2)]
damping = 0.5


def with_halo(cells, sides, width):
    for axis, dim in sides:
        count = lax.axis_size(axis)
        ends = count - 1
        head = lax.slice_in_dim(cells, 0, width, axis=dim)
        tail = lax.slice_in_dim(cells, cells.shape[dim] - width, cells.shape[dim], axis=dim)
        cells = jnp.concatenate(
            [
                lax.ppermute(tail, axis, [(i, (i + 1) % count) for i in range(ends)]),
                cells,
                lax.ppermute(head, axis, [((i + 1) % count, i) for i in range(ends)]),
            ],
            axis=dim,
        )
    return cells


def from_behind(array, axis, by):
    size = lax.axis_size(axis)
    pairs = [(i, i + by) for i in range(size) if 0 <= i + by < size]
    return lax.ppermute(array, axis, pairs)


def cholesky_solve5(normal, rhs_terms, prior_diag):
    matrix = {}
    for number, pair_at in enumerate(param_pairs):
        matrix[pair_at] = normal[number]
        matrix[pair_at[1], pair_at[0]] = normal[number]
    for number in range(5):
        matrix[number, number] = matrix[number, number] + prior_diag[number]
    factor = {}
    for row_at in range(5):
        for col_at in range(row_at + 1):
            running = matrix[row_at, col_at]
            for inner_k in range(col_at):
                running = running - factor[row_at, inner_k] * factor[col_at, inner_k]
            if row_at == col_at:
                factor[row_at, row_at] = jnp.sqrt(running)
            else:
                factor[row_at, col_at] = running / factor[col_at, col_at]
    forward = []
    for row_at in range(5):
        running = rhs_terms[row_at]
        for inner_k in range(row_at):
            running = running - factor[row_at, inner_k] * forward[inner_k]
        forward.append(running / factor[row_at, row_at])
    backward = [None] * 5
    for row_at in reversed(range(5)):
        running = forward[row_at]
        for inner_k in range(row_at + 1, 5):
            running = running - factor[inner_k, row_at] * backward[inner_k]
        backward[row_at] = running / factor[row_at, row_at]
    return jnp.stack(backward)


def spline_basis(local_time):
    floor_part = jnp.floor(local_time)
    frac_part = local_time - floor_part
    square = frac_part * frac_part
    cube_term = square * frac_part
    rest = 1.0 - frac_part
    splines = [
        rest * rest * rest / 6.0,
        (3.0 * cube_term - 6.0 * square + 4.0) / 6.0,
        (-3.0 * cube_term + 3.0 * square + 3.0 * frac_part + 1.0) / 6.0,
        cube_term / 6.0,
    ]
    return (floor_part.astype(jnp.int32), splines)


def band_sums(direction, pair_weight, rhs_vec, local_time, knots):
    floor_at, splines = spline_basis(local_time)
    knot_ids = jnp.arange(knots + 3, dtype=jnp.int32)
    outer_terms = []
    for left_at, right_at in sym_pairs:
        entry_term = direction[left_at] * direction[right_at]
        entry_term = pair_weight * entry_term
        outer_terms.append(entry_term)
    total = None
    for spline_at in range(4):
        choice_mask = (floor_at[..., None] + spline_at == knot_ids).astype(jnp.float32)
        column_list = []
        for offset in range(4 - spline_at):
            coeff_pair = splines[spline_at] * splines[spline_at + offset]
            for entry_term in outer_terms:
                column_list.append(coeff_pair * entry_term)
        scaled = rhs_vec * splines[spline_at]
        for axis_at in range(3):
            column_list.append(scaled * direction[axis_at])
        accumulated_sum = jnp.einsum(
            "gyf,yfm->gym", jnp.stack(column_list), choice_mask, precision=lax.Precision.HIGHEST
        )
        lead = 6 * (4 - spline_at)
        blank = jnp.zeros((6 * spline_at,) + accumulated_sum.shape[1:], jnp.float32)
        filled = jnp.concatenate([accumulated_sum[:lead], blank, accumulated_sum[lead:]], 0)
        total = filled if total is None else total + filled
    return (total, floor_at, splines)


def sym_apply(entries, vector):
    first_row = entries[0] * vector[0] + entries[1] * vector[1] + entries[2] * vector[2]
    middle_row_entries = entries[1] * vector[0] + entries[3] * vector[1] + entries[4] * vector[2]
    third_row = entries[2] * vector[0] + entries[4] * vector[1] + entries[5] * vector[2]
    return jnp.stack([first_row, middle_row_entries, third_row])


def symmetric_inverse(entries):
    cof_00 = entries[3] * entries[5] - entries[4] * entries[4]
    cof_01 = entries[2] * entries[4] - entries[1] * entries[5]
    cof_02 = entries[1] * entries[4] - entries[2] * entries[3]
    cof_11 = entries[0] * entries[5] - entries[2] * entries[2]
    cof_12 = entries[1] * entries[2] - entries[0] * entries[4]
    cof_22 = entries[0] * entries[3] - entries[1] * entries[1]
    determinant = entries[0] * cof_00 + entries[1] * cof_01 + entries[2] * cof_02
    return jnp.stack([cof_00, cof_01, cof_02, cof_11, cof_12, cof_22]) / determinant


def add_prior(diag_sums, prior_diag):
    return jnp.stack(
        [
            diag_sums[0] + prior_diag[0],
            diag_sums[1],
            diag_sums[2],
            diag_sums[3] + prior_diag[1],
            diag_sums[4],
            diag_sums[5] + prior_diag[2],
        ]
    )


def apply_operator(diag_block, upper_triangle_filled, vector_padded, knot_count):
    applied = sym_apply(diag_block, vector_padded[:, 3 : 3 + knot_count])
    for offset in range(1, 4):
        upper_here = upper_triangle_filled[6 * (offset - 1) : 6 * offset, 3 : 3 + knot_count]
        upper_left = upper_triangle_filled[
            6 * (offset - 1) : 6 * offset, 3 - offset : 3 - offset + knot_count
        ]
        applied = applied + sym_apply(
            upper_here, vector_padded[:, 3 + offset : 3 + offset + knot_count]
        )
        applied = applied + sym_apply(
            upper_left, vector_padded[:, 3 - offset : 3 - offset + knot_count]
        )
    return applied


def body(
    residual,
    obs_weight,
    time_frac,
    src_partials,
    att_dir,
    src_prior,
    att_prior,
    obs_source,
    obs_interval,
    obs_count,
):
    src_count = lax.axis_size("src")
    seg_count = lax.axis_size("seg")
    obs_local = residual.shape[0]
    capacity = obs_local // src_count
    sources = src_prior.shape[1]
    knots = att_prior.shape[1]
    seg_at = lax.axis_index("seg")
    slot_ok = jnp.arange(capacity, dtype=jnp.int32)[None, :] < obs_count[0][:, None]
    live_mask = slot_ok.reshape(-1).astype(jnp.float32)
    weight = obs_weight * live_mask
    features = []
    for left_at, right_at in param_pairs:
        features.append(weight * src_partials[left_at] * src_partials[right_at])
    for axis_at in range(5):
        features.append(weight * src_partials[axis_at] * residual)
    src_sums = jax.ops.segment_sum(jnp.stack(features, 1), obs_source, num_segments=sources).T
    share_cols = sources // seg_count
    part_sums = lax.psum_scatter(src_sums, "seg", scatter_dimension=1, tiled=True)
    part_prior = lax.dynamic_slice_in_dim(src_prior, seg_at * share_cols, share_cols, 1)
    part_update = cholesky_solve5(part_sums[:15], part_sums[15:], part_prior)
    src_update = lax.all_gather(part_update, "seg", axis=1, tiled=True)
    src_corr = jnp.sum(src_partials * jnp.take(src_update, obs_source, axis=1), 0)
    first_pass = residual - src_corr
    local_time = (obs_interval % knots).astype(jnp.float32) + time_frac
    packed = jnp.stack(
        [first_pass, weight, local_time, att_dir[0], att_dir[1], att_dir[2]]
    ).reshape(6, src_count, capacity)
    incoming_values = lax.all_to_all(packed, "src", split_axis=1, concat_axis=1, tiled=True)
    arrived = incoming_values.reshape(6, 1, obs_local)
    band_total, arrived_floor, arrived_splines = band_sums(
        arrived[3:6], arrived[1], arrived[1] * arrived[0], arrived[2], knots
    )
    ext_sums = band_total[:, 0, :]
    zero_col = jnp.zeros((27,), jnp.float32)
    edge_cols = jnp.stack(
        [ext_sums[:, 0], zero_col, ext_sums[:, knots + 1], ext_sums[:, knots + 2]], 1
    )
    edge_rims = with_halo(edge_cols, ((("src", "seg"), 1),), 2)
    own_sums = ext_sums[:, 1 : knots + 1]
    own_sums = own_sums.at[:, 0:2].add(edge_rims[:, 0:2])
    own_sums = own_sums.at[:, knots - 1].add(edge_rims[:, 6])
    diag_block = add_prior(own_sums[:6], att_prior)
    inverse = symmetric_inverse(diag_block)
    att_rhs = own_sums[24:27]
    lower_rim = from_behind(own_sums[6:24, knots - 3 : knots], ("src", "seg"), 1)
    upper_triangle_filled = jnp.concatenate([lower_rim, own_sums[6:24]], 1)
    att_update = damping * sym_apply(inverse, att_rhs)
    for sweep_at in range(1, ITERS_ATT):
        vector_padded = with_halo(att_update, ((("src", "seg"), 1),), 3)
        att_update = att_update + damping * sym_apply(
            inverse,
            att_rhs - apply_operator(diag_block, upper_triangle_filled, vector_padded, knots),
        )
    final_padded = with_halo(att_update, ((("src", "seg"), 1),), 3)
    arrived_dir = arrived[3:6, 0]
    correction = jnp.zeros((obs_local,), jnp.float32)
    for spline_at in range(4):
        looked = jnp.take(final_padded, arrived_floor[0] + spline_at + 2, axis=1)
        correction = correction + arrived_splines[spline_at][0] * jnp.sum(arrived_dir * looked, 0)
    returned = lax.all_to_all(
        correction.reshape(src_count, capacity), "src", split_axis=0, concat_axis=0, tiled=True
    )
    att_corr = returned.reshape(-1)
    residual_out = residual - live_mask * (src_corr + att_corr)
    return (src_update, att_update, residual_out)


def solution(mesh):
    in_specs = (
        P(("src", "seg")),
        P(("src", "seg")),
        P(("src", "seg")),
        P(None, ("src", "seg")),
        P(None, ("src", "seg")),
        P(None, "src"),
        P(None, ("src", "seg")),
        P(("src", "seg")),
        P(("src", "seg")),
        P(("src", "seg"), None),
    )
    out_specs = (P(None, "src"), P(None, ("src", "seg")), P(("src", "seg")))
    return jax.shard_map(body, mesh=mesh, in_specs=in_specs, out_specs=out_specs, check_vma=False)
```

profile of v0, /device:TPU:0, one launch (start us, length us, event | category | flops | bytes accessed | tf_op | source)
XLA Modules:
  0.0 576.7 jit_solution(18023081326603989527)
XLA Ops:
  8.0 2.4 fusion.167
  10.4 0.9 multiply_multiply_fusion.11
  11.3 0.9 multiply_multiply_fusion.14
  12.3 2.1 stack.170
  14.4 4.8 copy.96
  19.2 87.9 %scatter_custom_fusion = f32[2048,20]{1,0:T(8,128)S(1)} fusion(s32[16384]{0:T(1024)S(1)} %copy-done.2, f32[16384,20]{1,0:T(8,128)} %copy.96, f32[]{:T(128)} %constant.122.clone.1), kind=kCustom, calls=%fused_computation.49 | custom fusion | flops 327680 | bytes 164352 | tf_op jit(solution)/shard_map/scatter-add | solution.py:203
  107.1 1.0 copy.97
  108.2 5.3 copy.99
  113.6 17.1 %reduce-scatter.2.cloned.1.call-done = f32[20,512]{1,0:T(8,128)} async-done(((f32[20,2048]{1,0:T(8,128)}), f32[20,512]{1,0:T(8,128)}) %reduce-scatter.2.cloned.1.call-update) | async-done | bytes 40976 | tf_op jit(solution)/shard_map/reduce_scatter | solution.py:205
  130.7 1.1 fusion.151
  132.7 0.9 subtract_divide_fusion
  133.7 5.2 all_gather.3
  139.3 54.5 %gather_fusion = f32[16384,5]{1,0:T(8,128)} fusion(f32[5,2048]{0,1:T(8,128)S(1)} %copy.98, s32[16384]{0:T(1024)S(1)} %fusion.87), kind=kCustom, calls=%fused_computation.4 | custom fusion | bytes 720896 | tf_op jit(solution)/shard_map/jit(_take)/gather | solution.py:209
  193.8 7.5 %fusion.4 = f32[16384]{0:T(1024)S(1)} fusion(f32[5,16384]{0,1:T(8,128)} %copy.99, f32[16384,5]{1,0:T(8,128)} %gather_fusion, pred[16384]{0:T(1024)(128)(4,1)S(1)} %compare_and_fusion.4), kind=kLoop, calls=%fused_computation.15 | loop fusion | flops 229376 | bytes 737280 | tf_op jit(solution)/shard_map/reduce_sum | solution.py:209
  201.3 1.0 pad_maximum_fusion
  202.4 5.5 all-to-all-start
  208.9 14.0 %all-to-all-done = f32[6,8,2048]{2,0,1:T(8,128)S(1)} async-done(((f32[6,8,2048]{2,0,1:T(8,128)}), f32[6,8,2048]{2,0,1:T(8,128)S(1)}, u32[]{:S(2)}, u32[]{:S(2)}) %all-to-all-start) | async-done | bytes 393248 | tf_op jit(solution)/shard_map/all_to_all | solution.py:215
  229.2 2.5 fusion.55
  231.7 2.6 fusion.58
  234.4 3.0 fusion.50
  237.4 3.1 fusion.45
  240.7 1.3 collective-permute-start
  242.0 1.3 collective-permute-start.1
  243.4 4.7 copy.104
  249.6 3.9 collective-permute-start.4
  253.5 1.3 collective-permute-start.2
  254.8 4.3 collective-permute-start.3
  260.5 3.6 collective-permute-start.6
  264.2 1.3 collective-permute-start.5
  265.5 3.5 collective-permute-done.5
  269.6 4.4 collective-permute-start.8
  274.1 1.3 collective-permute-start.7
  275.4 3.8 collective-permute-done.7
  279.8 5.8 collective-permute-start.10
  285.6 1.3 collective-permute-start.9
  286.9 1.7 collective-permute-done.9
  289.3 4.7 collective-permute-start.12
  294.0 1.3 collective-permute-start.11
  295.3 1.7 collective-permute-done.11
  297.7 5.4 collective-permute-start.13
  303.1 1.3 collective-permute-start.14
  304.4 1.7 collective-permute-done.14
  306.3 54.5 %gather_fusion.4 = f32[16384,3]{1,0:T(8,128)} fusion(f32[3,70]{0,1:T(8,128)S(1)} %copy.105, s32[16384]{0:T(1024)S(1)} %get-tuple-element.191), kind=kCustom, calls=%fused_computation.3.clone | custom fusion | bytes 458752 | tf_op jit(solution)/shard_map/jit(_take)/gather | solution.py:245
  360.8 54.5 %gather_fusion.3 = f32[16384,3]{1,0:T(8,128)} fusion(f32[3,70]{0,1:T(8,128)S(1)} %copy.105, s32[16384]{0:T(1024)S(1)} %get-tuple-element.192), kind=kCustom, calls=%fused_computation.2.clone | custom fusion | bytes 458752 | tf_op jit(solution)/shard_map/jit(_take)/gather | solution.py:245
  415.3 54.5 %gather_fusion.2 = f32[16384,3]{1,0:T(8,128)} fusion(f32[3,70]{0,1:T(8,128)S(1)} %copy.105, s32[16384]{0:T(1024)S(1)} %get-tuple-element.190), kind=kCustom, calls=%fused_computation.1.clone | custom fusion | bytes 458752 | tf_op jit(solution)/shard_map/jit(_take)/gather | solution.py:245
  469.7 54.5 %gather_fusion.1 = f32[16384,3]{1,0:T(8,128)} fusion(f32[3,70]{0,1:T(8,128)S(1)} %copy.105, s32[16384]{0:T(1024)S(1)} %get-tuple-element.189), kind=kCustom, calls=%fused_computation.clone | custom fusion | bytes 458752 | tf_op jit(solution)/shard_map/jit(_take)/gather | solution.py:245
  524.2 26.1 %fusion = (f32[16384]{0:T(1024)S(1)}, f32[16384]{0:T(1024)S(1)}, f32[16384]{0:T(1024)S(1)}, f32[16384]{0:T(1024)S(1)}) fusion(f32[3,8,2048]{0,2,1:T(8,128)} %copy.104, f32[16384,3]{1,0:T(8,128)} %gather_fusion.4, pred[16384]{0:T(1024)(128)(4,1)S(1)} %get-tuple-element.187, f32[16384,3]{1,0:T(8,128)} %gather_fusion.2, ...), kind=kLoop, calls=%fused_computation.7 | loop fusion | flops 524288 | bytes 1310720 | tf_op jit(solution)/shard_map/reduce_sum | solution.py:246
  550.6 18.0 %all_to_all.11 = f32[8,1,2048]{2,1,0:T(1,128)S(1)} all-to-all(f32[8,1,2048]{2,1,0:T(1,128)S(1)} %copy.109), channel_id=1, replica_groups=mesh['src'=8,'seg'=4] {'src'}, dimensions={0} | all-to-all | bytes 131072 | tf_op jit(solution)/shard_map/all_to_all | solution.py:247
  (183 shorter events, 16.5 us)
Async XLA Ops:
  7.2 123.6 %reduce-scatter.2.cloned.1.call-start = ((), (), s32[]{:S(2)}) async-start(), calls=%async_computation.3 | async-start | bytes 245760 | tf_op jit(solution)/shard_map/reduce_scatter | solution.py:205
  14.4 4.8 copy-start.2
  19.2 89.0 %copy-start = (f32[5,16384]{1,0:T(8,128)S(1)}, f32[5,16384]{1,0:T(8,128)}, u32[]{:S(2)}) copy-start(f32[5,16384]{1,0:T(8,128)} %param.19) | copy-start | bytes 983044
  108.2 5.3 copy-start.4
  108.2 5.3 copy-start.5
  193.7 7.6 %copy-start.1 = (f32[16384]{0:T(1024)S(1)}, f32[16384]{0:T(1024)}, u32[]{:S(2)}) copy-start(f32[16384]{0:T(1024)} %param.16) | copy-start | bytes 196612
  193.7 7.6 %copy-start.3 = (f32[3,16384]{1,0:T(4,128)S(1)}, f32[3,16384]{1,0:T(4,128)}, u32[]{:S(2)}) copy-start(f32[3,16384]{1,0:T(4,128)} %param.20) | copy-start | bytes 589828
  202.4 20.5 %all-to-all-start = ((f32[6,8,2048]{2,0,1:T(8,128)}), f32[6,8,2048]{2,0,1:T(8,128)S(1)}, u32[]{:S(2)}, u32[]{:S(2)}) async-start(f32[6,8,2048]{2,0,1:T(8,128)} %pad_maximum_fusion), calls=%async_computation.1 | async-start | bytes 1048576 | tf_op jit(solution)/shard_map/all_to_all | solution.py:215
  234.4 6.3 %copy-start.8 = (pred[2]{0:T(512)(128)(4,1)S(1)}, pred[2]{0:T(512)(128)(4,1)}, u32[]{:S(2)}) copy-start(pred[2]{0:T(512)(128)(4,1)} %constant.142.clone.1) | copy-start | bytes 10
  240.7 7.4 %collective-permute-start = (f32[27,2]{1,0:T(8,128)S(1)}, f32[27,2]{1,0:T(8,128)S(1)}, u32[]{:S(2)}, u32[]{:S(2)}) collective-permute-start(f32[27,2]{1,0:T(8,128)S(1)} %get-tuple-element.315), channel_id=1, source_target_pairs={{0,1},{1,2},{2,3},{3,4},{4,5},{5,6},{6,7},{7,8},{8,9},{9,10},{10,1... | collective-permute-start | bytes 656 | tf_op jit(solution)/shard_map/ppermute | solution.py:38
  242.0 7.1 %collective-permute-start.1 = (f32[27,2]{1,0:T(8,128)S(1)}, f32[27,2]{1,0:T(8,128)S(1)}, u32[]{:S(2)}, u32[]{:S(2)}) collective-permute-start(f32[27,2]{1,0:T(8,128)S(1)} %get-tuple-element.314), channel_id=1, source_target_pairs={{1,0},{2,1},{3,2},{4,3},{5,4},{6,5},{7,6},{8,7},{9,8},{10,9},{11,1... | collective-permute-start | bytes 656 | tf_op jit(solution)/shard_map/ppermute | solution.py:40
  243.4 5.9 %copy-start.7 = (f32[3,64]{1,0:T(4,128)S(1)}, f32[3,64]{1,0:T(4,128)}, u32[]{:S(2)}) copy-start(f32[3,64]{1,0:T(4,128)} %param.22) | copy-start | bytes 2308
  249.6 9.5 %collective-permute-start.4 = (f32[3,3]{1,0:T(4,128)S(1)}, f32[3,3]{1,0:T(4,128)S(1)}, u32[]{:S(2)}, u32[]{:S(2)}) collective-permute-start(f32[3,3]{1,0:T(4,128)S(1)} %get-tuple-element.387), channel_id=1, source_target_pairs={{0,1},{1,2},{2,3},{3,4},{4,5},{5,6},{6,7},{7,8},{8,9},{9,10},{10,1... | collective-permute-start | bytes 116 | tf_op jit(solution)/shard_map/ppermute | solution.py:38
  253.5 5.6 collective-permute-start.2
  254.8 5.1 collective-permute-start.3
  260.5 4.9 collective-permute-start.6
  264.2 4.8 collective-permute-start.5
  269.6 5.7 collective-permute-start.8
  274.1 5.1 collective-permute-start.7
  279.8 7.1 %collective-permute-start.10 = (f32[3,3]{1,0:T(4,128)S(1)}, f32[3,3]{1,0:T(4,128)S(1)}, u32[]{:S(2)}, u32[]{:S(2)}) collective-permute-start(f32[3,3]{1,0:T(4,128)S(1)} %get-tuple-element.375), channel_id=1, source_target_pairs={{0,1},{1,2},{2,3},{3,4},{4,5},{5,6},{6,7},{7,8},{8,9},{9,10},{10,1... | collective-permute-start | bytes 116 | tf_op jit(solution)/shard_map/ppermute | solution.py:38
  285.6 3.1 collective-permute-start.9
  289.3 6.0 %collective-permute-start.12 = (f32[3,3]{1,0:T(4,128)S(1)}, f32[3,3]{1,0:T(4,128)S(1)}, u32[]{:S(2)}, u32[]{:S(2)}) collective-permute-start(f32[3,3]{1,0:T(4,128)S(1)} %get-tuple-element.371), channel_id=1, source_target_pairs={{0,1},{1,2},{2,3},{3,4},{4,5},{5,6},{6,7},{7,8},{8,9},{9,10},{10,1... | collective-permute-start | bytes 116 | tf_op jit(solution)/shard_map/ppermute | solution.py:38
  294.0 3.1 collective-permute-start.11
  297.6 117.7 %copy-start.6 = (f32[3,64]{1,0:T(4,128)}, f32[3,64]{1,0:T(4,128)S(1)}, u32[]{:S(2)}) copy-start(f32[3,64]{1,0:T(4,128)S(1)} %fusion.148) | copy-start | bytes 2308
  297.7 6.7 %collective-permute-start.13 = (f32[3,3]{1,0:T(4,128)S(1)}, f32[3,3]{1,0:T(4,128)S(1)}, u32[]{:S(2)}, u32[]{:S(2)}) collective-permute-start(f32[3,3]{1,0:T(4,128)S(1)} %get-tuple-element.367), channel_id=1, source_target_pairs={{0,1},{1,2},{2,3},{3,4},{4,5},{5,6},{6,7},{7,8},{8,9},{9,10},{10,1... | collective-permute-start | bytes 116 | tf_op jit(solution)/shard_map/ppermute | solution.py:38
  303.1 3.1 collective-permute-start.14
Sparse Core Ops, SparseCore 0:
  108.3 22.4 reduce-scatter.1
where the time goes:
time: 578 us; the launch traced here: 577 us
  local copies, waits for them, and re-layouts  296 us (51%)
  other arithmetic  139 us (24%)
  starting transfers between devices  47.9 us (8%)
  waiting for transfers between devices  44.2 us (8%)
  blocking collectives  23.3 us (4%)
  between operations  15 us (3%)
  matrix products  11.2 us (2%)
    gather x4, local copies, waits for them, and re-layouts, body(): looked = jnp.take(final_padded, arrived_floor[0] + spline_at + 2, axis=1)  218 us
    scatter-add x1, other arithmetic, body(): jax.ops.segment_sum(jnp.stack(features, 1), obs_source, num_segments=sour...  87.9 us
    gather x1, local copies, waits for them, and re-layouts, body(): jnp.take(src_update, obs_source, axis=1)  54.5 us
    ppermute x7, starting transfers between devices, with_halo(): lax.ppermute(tail, axis, [(i, (i + 1) % count) for i in range(ends)])  29.1 us
    reduce_sum x1, other arithmetic, body(): jnp.sum(arrived_dir * looked, 0)  26.1 us
    all_to_all x1, blocking collectives, body(): lax.all_to_all(correction.reshape(src_count, capacity), 'src', split_axis...  18 us
    reduce_scatter x1, waiting for transfers between devices, body(): lax.psum_scatter(src_sums, 'seg', scatter_dimension=1, tiled=True)  17.1 us
    all_to_all x1, waiting for transfers between devices, body(): lax.all_to_all(packed, 'src', split_axis=1, concat_axis=1, tiled=True)  14 us
  transfers between devices with their start and end apart: 17, of which 8 were waited for; matrix products, arithmetic and copies ran while one was open for 2% of the time, Pallas kernels for 0%

commit v1 on v0

v1 whole, which is shorter than its diff:
```python
import functools

import jax
import jax.numpy as jnp
from jax import lax
from jax.experimental import pallas as pl
from jax.experimental.pallas import tpu as pltpu
from jax.sharding import PartitionSpec as P

ITERS_ATT = 6
LO = 256
LANES = 128
F32 = jnp.float32
BF16 = jnp.bfloat16
PAIR_ROW = {}
for _d in range(3):
    for _p in range(5):
        _q = (_p + _d) % 5
        PAIR_ROW[_p, _q] = 5 * _d + _p
        PAIR_ROW[_q, _p] = 5 * _d + _p
damping = 0.5
vmem = pl.BlockSpec(memory_space=pltpu.VMEM)
smem = pl.BlockSpec(memory_space=pltpu.SMEM)


def split_rows(values):
    high = values.astype(BF16).astype(F32)
    return jnp.concatenate([high, values - high], 0).astype(BF16)


def contract_lanes(left, right):
    return lax.dot_general(left, right, (((1,), (1,)), ((), ())), preferred_element_type=F32)


def matmul(left, right):
    return lax.dot_general(left, right, (((1,), (0,)), ((), ())), preferred_element_type=F32)


def one_hot(index_row, rows):
    ids = lax.broadcasted_iota(jnp.int32, (rows, index_row.shape[1]), 0)
    return jnp.where(ids == index_row, 1.0, 0.0).astype(BF16)


def live_weight(weight_row, count):
    place = lax.broadcasted_iota(jnp.int32, weight_row.shape, 1)
    return jnp.where(place < count, weight_row, 0.0)


def basis(interval_row, frac_row, knots):
    local_time = (interval_row % knots).astype(F32) + frac_row
    floor_part = jnp.floor(local_time)
    u = local_time - floor_part
    square = u * u
    cube = square * u
    rest = 1.0 - u
    splines = [
        rest * rest * rest / 6.0,
        (3.0 * cube - 6.0 * square + 4.0) / 6.0,
        (-3.0 * cube + 3.0 * square + 3.0 * u + 1.0) / 6.0,
        cube / 6.0,
    ]
    return floor_part.astype(jnp.int32), splines


def source_sums_block(partials, weight, residual, source, hot):
    width = partials.shape[1]
    weighted = partials * weight
    features = jnp.concatenate(
        [
            weighted * partials,
            weighted * jnp.concatenate([partials[1:], partials[:1]], 0),
            weighted * jnp.concatenate([partials[2:], partials[:2]], 0),
            weighted * residual,
            jnp.zeros((4, width), F32),
        ],
        0,
    )
    return split_rows(features)


def expand(split, high_row, groups):
    width = split.shape[1]
    high16 = jnp.broadcast_to(high_row, (16, width))
    parts = []
    for group in range(groups):
        mask = jnp.where(high16 == group, 1.0, 0.0).astype(BF16)
        for start in range(0, split.shape[0], 16):
            parts.append(split[start : start + 16] * mask)
    return jnp.concatenate(parts, 0)


def normal_block(direction, weight, splines, hot):
    blank = jnp.zeros((2, direction.shape[1]), F32)
    d0, d1, d2 = direction[0:1], direction[1:2], direction[2:3]
    entries = (
        weight
        * jnp.concatenate([d0, d0, d0, d1, d1, d2, blank], 0)
        * jnp.concatenate([d0, d1, d2, d1, d2, d2, blank], 0)
    )
    groups = []
    for at in range(4):
        for offset in range(4 - at):
            groups.append((splines[at] * splines[at + offset]) * entries)
    rows = 8 * len(groups)
    sums = contract_lanes(split_rows(jnp.concatenate(groups, 0)), hot)
    sums = sums[:rows] + sums[rows:]
    upper = [None] * 4
    number = 0
    for at in range(4):
        for offset in range(4 - at):
            term = sums[8 * number : 8 * number + 8]
            term = term if at == 0 else pltpu.roll(term, at, 1)
            upper[offset] = term if upper[offset] is None else upper[offset] + term
            number += 1
    return jnp.concatenate([term[:6] for term in upper], 0)


def rhs_block(direction, weighted_first, splines, hot):
    base = jnp.concatenate(
        [direction * weighted_first, jnp.zeros((5, direction.shape[1]), F32)], 0
    )
    sums = contract_lanes(split_rows(jnp.concatenate([s * base for s in splines], 0)), hot)
    sums = sums[:32] + sums[32:]
    total = sums[:8]
    for at in range(1, 4):
        total = total + pltpu.roll(sums[8 * at : 8 * at + 8], at, 1)
    return total


def cholesky_solve5(sums, prior):
    factor = {}
    for row in range(5):
        for col in range(row + 1):
            at = PAIR_ROW[row, col]
            running = sums[at : at + 1]
            if row == col:
                running = running + prior[row : row + 1]
            for k in range(col):
                running = running - factor[row, k] * factor[col, k]
            if row == col:
                factor[row, row] = jnp.sqrt(running)
            else:
                factor[row, col] = running / factor[col, col]
    forward = []
    for row in range(5):
        running = sums[15 + row : 16 + row]
        for k in range(row):
            running = running - factor[row, k] * forward[k]
        forward.append(running / factor[row, row])
    backward = [None] * 5
    for row in reversed(range(5)):
        running = forward[row]
        for k in range(row + 1, 5):
            running = running - factor[k, row] * backward[k]
        backward[row] = running / factor[row, row]
    return jnp.concatenate(backward + [jnp.zeros((3, LO), F32)], 0)


def source_lookup(table, hot, high_row, partials):
    groups = table.shape[0] // 16
    looked = matmul(table, hot)
    half = 8 * groups
    high8 = jnp.broadcast_to(high_row, (8, hot.shape[1]))
    chosen = None
    for group in range(groups):
        term = looked[8 * group : 8 * group + 8] + looked[half + 8 * group : half + 8 * group + 8]
        term = jnp.where(high8 == group, term, 0.0)
        chosen = term if chosen is None else chosen + term
    return jnp.sum(partials * chosen[:5], 0, keepdims=True)


def attitude_lookup(window, shift, hot, splines, direction):
    tables = [pltpu.roll(window, LANES - (shift + at), 1) for at in range(4)]
    looked = matmul(split_rows(jnp.concatenate(tables, 0)), hot)
    looked = looked[:32] + looked[32:]
    total = None
    for at in range(4):
        term = splines[at] * looked[8 * at : 8 * at + 3]
        total = term if total is None else total + term
    return jnp.sum(direction * total, 0, keepdims=True)


def sym_apply(e, v):
    return [
        e[0] * v[0] + e[1] * v[1] + e[2] * v[2],
        e[1] * v[0] + e[3] * v[1] + e[4] * v[2],
        e[2] * v[0] + e[4] * v[1] + e[5] * v[2],
    ]


def symmetric_inverse(e):
    c00 = e[3] * e[5] - e[4] * e[4]
    c01 = e[2] * e[4] - e[1] * e[5]
    c02 = e[1] * e[4] - e[2] * e[3]
    c11 = e[0] * e[5] - e[2] * e[2]
    c12 = e[1] * e[2] - e[0] * e[4]
    c22 = e[0] * e[3] - e[1] * e[1]
    det = e[0] * c00 + e[1] * c01 + e[2] * c02
    return [c / det for c in (c00, c01, c02, c11, c12, c22)]


def window_of(before, own, after, halo, knots):
    lane = lax.broadcasted_iota(jnp.int32, own.shape, 1)
    left = pltpu.roll(before, (halo - 1 - knots) % LANES, 1)
    right = pltpu.roll(after, (halo - 1 + knots) % LANES, 1)
    total = pltpu.roll(own, halo - 1, 1)
    total = total + jnp.where(lane < halo + 2, left, 0.0)
    return total + jnp.where(lane >= halo - 1 + knots, right, 0.0)


def knot_valid(me, halo, knots, total):
    lane = lax.broadcasted_iota(jnp.int32, (1, LANES), 1)
    knot = me * knots + lane - halo
    return (knot >= 0) & (knot < total)


def prepare(normals, valid):
    rows = [jnp.where(valid, normals[i : i + 1], 0.0) for i in range(24)]
    diag = [jnp.where(valid, rows[i], 1.0 if i in (0, 3, 5) else 0.0) for i in range(6)]
    inverse = [jnp.where(valid, x, 0.0) for x in symmetric_inverse(diag)]
    return diag, rows, inverse


def sweeps(diag, rows, inverse, rhs):
    update = [damping * x for x in sym_apply(inverse, rhs)]
    for _ in range(1, ITERS_ATT):
        applied = sym_apply(diag, update)
        for offset in range(1, 4):
            upper = rows[6 * offset : 6 * offset + 6]
            ahead = [pltpu.roll(x, LANES - offset, 1) for x in update]
            behind = [pltpu.roll(x, offset, 1) for x in sym_apply(upper, update)]
            for at, x in enumerate(sym_apply(upper, ahead)):
                applied[at] = applied[at] + x + behind[at]
        step = sym_apply(inverse, [rhs[at] - applied[at] for at in range(3)])
        update = [update[at] + damping * step[at] for at in range(3)]
    return update


def block_slice(block, width):
    return pl.ds(pl.multiple_of(block * width, 128), width)


def sums_kernel(knots, res, ow, tf, sp, ad, osrc, oint, cnt, out_sums, out_norm, acc):
    blocks = cnt.shape[1]
    width = res.shape[1] // blocks
    groups = out_sums.shape[0]
    acc[...] = jnp.zeros_like(acc)

    def step(block, carry):
        sl = block_slice(block, width)
        weight = live_weight(ow[:, sl], cnt[0, block])
        source = osrc[:, sl]
        hot = one_hot(source % LO, LO)
        split = source_sums_block(sp[:, sl], weight, res[:, sl], source, hot)
        acc[...] += contract_lanes(expand(split, source // LO, groups), hot)
        floor_at, splines = basis(oint[:, sl], tf[:, sl], knots)
        out_norm[block] = normal_block(ad[:, sl], weight, splines, one_hot(floor_at, LANES))
        return carry

    lax.fori_loop(0, blocks, step, 0)
    for group in range(groups):
        out_sums[group] = acc[48 * group : 48 * group + 24] + acc[48 * group + 24 : 48 * group + 48]


def solve_kernel(sums, prior, out):
    for group in range(sums.shape[0]):
        out[group] = cholesky_solve5(sums[group], prior[:, group * LO : (group + 1) * LO])


def first_kernel(knots, upd, res, ow, tf, sp, ad, osrc, oint, cnt, out_upd, out_corr, out_rhs):
    blocks = cnt.shape[1]
    width = res.shape[1] // blocks
    groups = upd.shape[0]
    for group in range(groups):
        out_upd[:, group * LO : (group + 1) * LO] = upd[group, :5]
    table = split_rows(jnp.concatenate([upd[group] for group in range(groups)], 0))

    def step(block, carry):
        sl = block_slice(block, width)
        weight = live_weight(ow[:, sl], cnt[0, block])
        source = osrc[:, sl]
        corr = source_lookup(table, one_hot(source % LO, LO), source // LO, sp[:, sl])
        out_corr[:, sl] = corr
        floor_at, splines = basis(oint[:, sl], tf[:, sl], knots)
        out_rhs[block] = rhs_block(
            ad[:, sl], weight * (res[:, sl] - corr), splines, one_hot(floor_at, LANES)
        )
        return carry

    lax.fori_loop(0, blocks, step, 0)


def sweep_kernel(knots, total, halo, before, own, after, out_window, out_own):
    me = lax.axis_index("src") * lax.axis_size("seg") + lax.axis_index("seg")
    window = window_of(before[...], own[...], after[...], halo, knots)
    valid = knot_valid(me, halo, knots, total)
    diag, rows, inverse = prepare(window, valid)
    rhs = [jnp.where(valid, window[24 + at : 25 + at], 0.0) for at in range(3)]
    update = sweeps(diag, rows, inverse, rhs)
    final = jnp.concatenate(update + [jnp.zeros((5, LANES), F32)], 0)
    out_window[...] = final
    out_own[...] = pltpu.roll(final, LANES - halo, 1)[:3, :knots]


def last_kernel(knots, halo, windows, corr, res, tf, ad, oint, cnt, out):
    blocks = cnt.shape[1]
    width = res.shape[1] // blocks

    def step(block, carry):
        sl = block_slice(block, width)
        floor_at, splines = basis(oint[:, sl], tf[:, sl], knots)
        att = attitude_lookup(
            windows[block], halo - 1, one_hot(floor_at, LANES), splines, ad[:, sl]
        )
        residual = res[:, sl]
        out[:, sl] = residual - live_weight(corr[:, sl] + att, cnt[0, block])
        return carry

    lax.fori_loop(0, blocks, step, 0)


def call(kernel, outs, n_vmem, count=False, scratch=()):
    return pl.pallas_call(
        kernel,
        out_shape=[jax.ShapeDtypeStruct(shape, F32) for shape in outs],
        in_specs=[vmem] * n_vmem + [smem] * count,
        out_specs=[vmem] * len(outs),
        scratch_shapes=list(scratch),
        compiler_params=pltpu.CompilerParams(vmem_limit_bytes=40 * 2**20),
    )


def body(residual, obs_weight, time_frac, src_partials, att_dir, src_prior, att_prior,
         obs_source, obs_interval, obs_count):
    n_src = lax.axis_size("src")
    n_seg = lax.axis_size("seg")
    seg_at = lax.axis_index("seg")
    obs = residual.shape[0]
    sources = src_prior.shape[1]
    knots = att_prior.shape[1]
    total = knots * n_src * n_seg
    groups = sources // LO
    halo = 32
    rows = [x.reshape(1, obs) for x in (residual, obs_weight, time_frac, obs_source, obs_interval)]
    res, ow, tf, osrc, oint = rows
    sums, normals = call(
        functools.partial(sums_kernel, knots),
        [(groups, 24, LO), (n_src, 24, LANES)], 7, True, [pltpu.VMEM((groups * 48, LO), F32)],
    )(res, ow, tf, src_partials, att_dir, osrc, oint, obs_count)
    part = lax.psum_scatter(sums, "seg", scatter_dimension=0, tiled=True)
    share = sources // n_seg
    prior = lax.dynamic_slice_in_dim(src_prior, seg_at * share, share, 1)
    (upd,) = call(solve_kernel, [(groups // n_seg, 8, LO)], 2)(part, prior)
    upd = lax.all_gather(upd, "seg", axis=0, tiled=True)
    src_update, corr, rhs = call(
        functools.partial(first_kernel, knots),
        [(5, sources), (1, obs), (n_src, 8, LANES)], 8, True,
    )(upd, res, ow, tf, src_partials, att_dir, osrc, oint, obs_count)
    sent = jnp.concatenate([normals, rhs], 1)
    own = jnp.sum(lax.all_to_all(sent, "src", split_axis=0, concat_axis=0, tiled=True), 0)
    prior_ext = jnp.pad(att_prior, ((0, 0), (1, LANES - 1 - knots)))
    own = own.at[0].add(prior_ext[0]).at[3].add(prior_ext[1]).at[5].add(prior_ext[2])
    count = n_src * n_seg
    before = lax.ppermute(own, ("src", "seg"), [(i, i + 1) for i in range(count - 1)])
    after = lax.ppermute(own, ("src", "seg"), [(i + 1, i) for i in range(count - 1)])
    window, att_update = call(
        functools.partial(sweep_kernel, knots, total, halo), [(8, LANES), (3, knots)], 3
    )(before, own, after)
    windows = lax.all_gather(window, "src", axis=0)
    (out,) = call(functools.partial(last_kernel, knots, halo), [(1, obs)], 6, True)(
        windows, corr, res, tf, att_dir, oint, obs_count
    )
    return src_update, att_update, out.reshape(obs)


def solution(mesh):
    both = P(("src", "seg"))
    wide = P(None, ("src", "seg"))
    in_specs = (both, both, both, wide, wide, P(None, "src"), wide, both, both,
                P(("src", "seg"), None))
    out_specs = (P(None, "src"), wide, both)
    return jax.shard_map(body, mesh=mesh, in_specs=in_specs, out_specs=out_specs, check_vma=False)
```

time: 578 us -> 121 us (0.21)
  local copies, waits for them, and re-layouts: 296 us -> 8.42 us
  other arithmetic: 139 us -> 0.25 us
  starting transfers between devices: 47.9 us -> 4.35 us
  blocking collectives: 23.3 us -> 49.4 us
  waiting for transfers between devices: 44.2 us -> 23.4 us
  Pallas kernels: 0 us -> 20.7 us
  matrix products: 11.2 us -> 0 us
    gather x5 -> x0, local copies, waits for them, and re-layouts: 272 us -> none  [the longest x4 218 us: body(): looked = jnp.take(final_padded, arrived_floor[0] + spline_at + 2, axis=1)]
    scatter-add x1 -> x0, other arithmetic: 87.9 us -> none  [body(): jax.ops.segment_sum(jnp.stack(features, 1), obs_source, num_segments=sour...]
    ppermute x15 -> x2, starting transfers between devices: 42.4 us -> 4.31 us  [the longest x1 3.03 us: body(): lax.ppermute(own, ('src', 'seg'), [(i, i + 1) for i in range(count - 1)])]
    reduce_sum x2 -> x1, other arithmetic: 33.6 us -> 0.01 us  [body(): jnp.sum(lax.all_to_all(sent, 'src', split_axis=0, concat_axis=0, tiled=Tr...]
    all_gather x1 -> x2, blocking collectives: 5.25 us -> 36.5 us  [the longest x1 31.3 us: body(): windows = lax.all_gather(window, 'src', axis=0)]
    pallas_call x0 -> x5, Pallas kernels: none -> 20.7 us  [the longest x1 8.31 us: body(): call(functools.partial(sums_kernel, knots), [(groups, 24, LO), (n_src, 24...]
    all_to_all x1 -> x0, waiting for transfers between devices: 14 us -> none  [body(): lax.all_to_all(packed, 'src', split_axis=1, concat_axis=1, tiled=True)]
    ppermute x15 -> x2, waiting for transfers between devices: 13.1 us -> 0.81 us  [the longest x1 0.81 us: body(): lax.ppermute(own, ('src', 'seg'), [(i, i + 1) for i in range(count - 1)])]
  transfers between devices with their start and end apart: 17 -> 3, of which waited for: 8 -> 2; matrix products, arithmetic and copies ran while one was open for 2% -> 0% of each run, Pallas kernels for 0% -> 0%
where the time goes in v1:
time: 121 us
  blocking collectives  49.4 us (41%)
  waiting for transfers between devices  23.4 us (19%)
  Pallas kernels  20.7 us (17%)
  between operations  14.2 us (12%)
  local copies, waits for them, and re-layouts  8.42 us (7%)
  starting transfers between devices  4.35 us (4%)
    all_gather x1, blocking collectives, body(): windows = lax.all_gather(window, 'src', axis=0)  31.3 us
    reduce_scatter x1, waiting for transfers between devices, body(): part = lax.psum_scatter(sums, 'seg', scatter_dimension=0, tiled=True)  22.5 us
    all_to_all x1, blocking collectives, body(): lax.all_to_all(sent, 'src', split_axis=0, concat_axis=0, tiled=True)  12.8 us
    unnamed x36, local copies, waits for them, and re-layouts  8.34 us
    pallas_call x1, Pallas kernels, body(): call(functools.partial(sums_kernel, knots), [(groups, 24, LO), (n_src, 24...  8.31 us
    pallas_call x1, Pallas kernels, body(): call(functools.partial(first_kernel, knots), [(5, sources), (1, obs), (n_...  6.95 us
    all_gather x1, blocking collectives, body(): upd = lax.all_gather(upd, 'seg', axis=0, tiled=True)  5.25 us
    pallas_call x1, Pallas kernels, body(): call(functools.partial(last_kernel, knots, halo), [(1, obs)], 6, True)  4.1 us
  transfers between devices with their start and end apart: 3, of which 2 were waited for; matrix products, arithmetic and copies ran while one was open for 0% of the time, Pallas kernels for 0%

profile of v1, /device:TPU:0, one launch (start us, length us, event | category | flops | bytes accessed | tf_op | source)
XLA Modules:
  0.0 120.6 jit_solution(18190741359733546472)
XLA Ops:
  7.2 0.0 copy-start
  7.2 0.0 reduce-scatter.2.cloned.1.call-start
  7.2 0.0 copy-start.16
  7.2 0.6 copy-done.16
  7.9 0.0 copy-start.1
  7.9 0.9 copy-done.1
  8.8 0.0 copy-start.3
  8.8 1.0 copy-done.3
  9.9 0.0 copy-start.5
  9.9 0.8 copy-done.5
  10.7 0.0 copy-start.7
  10.7 0.8 copy-done.7
  11.6 0.0 copy-start.9
  11.6 0.8 copy-done.9
  12.4 0.0 copy-start.11
  12.4 0.8 copy-done.11
  13.2 0.0 copy-start.13
  13.2 0.8 copy-done.13
  14.1 0.0 copy-start.4
  14.1 8.3 %shard_map.121 = (f32[8,24,256]{2,1,0:T(8,128)}, f32[8,24,128]{2,1,0:T(8,128)S(1)}) custom-call(f32[1,16384]{1,0:T(1,128)S(1)} %bitcast.7, f32[1,16384]{1,0:T(1,128)S(1)} %bitcast.16, f32[1,16384]{1,0:T(1,128)S(1)} %bitcast.10, f32[5,16384]{1,0:T(8,128)S(1)} %copy-done.3, f32[3,16384]{1,0:T(4,128)S(1)} %copy-done.1, s32[1,16384]{1,0:T(1,128)S(1)} %bitcast.18, ...), custom_call_target="tpu_custom_call" | custom-call | tf_op jit(solution)/shard_map/pallas_call | solution.py:346
  22.4 0.0 reduce-scatter.2.cloned.1.call-update
  22.4 0.0 copy-done
  22.5 0.0 copy-start.6
  22.5 0.0 copy-start.8
  22.5 22.5 %reduce-scatter.2.cloned.1.call-done.sums = f32[2,24,256]{2,1,0:T(8,128)} async-done(((f32[8,24,256]{2,1,0:T(8,128)}), f32[2,24,256]{2,1,0:T(8,128)}) %reduce-scatter.2.cloned.1.call-update) | async-done | bytes 49168 | tf_op jit(solution)/shard_map/reduce_scatter | solution.py:350
  45.0 0.8 copy-done.15
  45.8 0.2 shard_map.122
  46.0 5.2 %all_gather.9.upd = f32[8,8,256]{2,1,0:T(8,128)S(1)} all-gather(f32[2,8,256]{2,1,0:T(8,128)S(1)} %shard_map.122), channel_id=1, replica_groups=mesh['src'=8,'seg'=4] {'seg'}, dimensions={0}, use_global_device_ids=true | all-gather | bytes 81920 | tf_op jit(solution)/shard_map/all_gather | solution.py:354
  51.2 0.0 copy-done.4
  51.2 0.0 copy-done.10
  51.2 0.0 copy-done.12
  51.2 0.0 copy-done.14
  51.2 0.0 copy-done.2
  51.3 0.0 copy-done.6
  51.3 0.0 copy-done.8
  51.3 6.9 %shard_map.123 = (f32[5,2048]{1,0:T(8,128)}, f32[1,16384]{1,0:T(1,128)S(1)}, f32[8,8,128]{2,1,0:T(8,128)S(1)}) custom-call(f32[8,8,256]{2,1,0:T(8,128)S(1)} %all_gather.9.upd, f32[1,16384]{1,0:T(1,128)S(1)} %bitcast.8, f32[1,16384]{1,0:T(1,128)S(1)} %bitcast.17, f32[1,16384]{1,0:T(1,128)S(1)} %bitcast.11, f32[5,16384]{1,0:T(8,128)S(1)} %copy-done.4, ...), custom_call_target="tpu_custom_call" | custom-call | tf_op jit(solution)/shard_map/pallas_call | solution.py:355
  58.2 12.8 %all_to_all.5 = f32[8,32,128]{2,1,0:T(8,128)S(1)} all-to-all(f32[8,32,128]{2,1,0:T(8,128)S(1)} %pad_maximum_fusion), channel_id=1, replica_groups=mesh['src'=8,'seg'=4] {'src'}, dimensions={0} | all-to-all | bytes 262144 | tf_op jit(solution)/shard_map/all_to_all | solution.py:360
  71.1 0.7 copy-done.17
  71.7 0.1 fusion
  71.8 0.1 fusion.1
  71.9 0.1 fusion.2
  72.0 1.3 %collective-permute-start.1 = (f32[32,128]{1,0:T(8,128)S(1)}, f32[32,128]{1,0:T(8,128)S(1)}, u32[]{:S(2)}, u32[]{:S(2)}) collective-permute-start(f32[32,128]{1,0:T(8,128)S(1)} %scatter-add.14.own), channel_id=1, source_target_pairs={{1,0},{2,1},{3,2},{4,3},{5,4},{6,5},{7,6},{8,7},{9,8},{10,9},{11,1... | collective-permute-start | bytes 49160 | tf_op jit(solution)/shard_map/ppermute | solution.py:365
  73.3 3.0 %collective-permute-start = (f32[32,128]{1,0:T(8,128)S(1)}, f32[32,128]{1,0:T(8,128)S(1)}, u32[]{:S(2)}, u32[]{:S(2)}) collective-permute-start(f32[32,128]{1,0:T(8,128)S(1)} %scatter-add.14.own), channel_id=1, source_target_pairs={{0,1},{1,2},{2,3},{3,4},{4,5},{5,6},{6,7},{7,8},{8,9},{9,10},{10,1... | collective-permute-start | bytes 49160 | tf_op jit(solution)/shard_map/ppermute | solution.py:364
  76.4 0.0 collective-permute-done.1.after
  76.4 0.8 collective-permute-done.before
  77.2 1.2 %shard_map.124 = (f32[8,128]{1,0:T(8,128)S(1)}, f32[3,64]{1,0:T(4,128)}) custom-call(f32[32,128]{1,0:T(8,128)S(1)} %collective-permute-done.before, f32[32,128]{1,0:T(8,128)S(1)} %scatter-add.14.own, f32[32,128]{1,0:T(8,128)S(1)} %collective-permute-done.1.after), custom_call_target="tpu_custom_call" | custom-call | tf_op jit(solution)/shard_map/pallas_call | solution.py:366
  78.4 31.3 %all-gather = f32[64,128]{1,0:T(8,128)S(1)} all-gather(f32[8,128]{1,0:T(8,128)S(1)} %get-tuple-element.51), channel_id=2, replica_groups=mesh['src'=8,'seg'=4] {'src'}, dimensions={0}, use_global_device_ids=true | all-gather | bytes 36864 | tf_op jit(solution)/shard_map/all_gather | solution.py:369
  109.7 4.1 %shard_map.125 = f32[1,16384]{1,0:T(1,128)} custom-call(f32[8,8,128]{2,1,0:T(8,128)S(1)} %bitcast.20, f32[1,16384]{1,0:T(1,128)S(1)} %get-tuple-element.52.corr, f32[1,16384]{1,0:T(1,128)S(1)} %bitcast.9, f32[1,16384]{1,0:T(1,128)S(1)} %bitcast.12, f32[3,16384]{1,0:T(4,128)S(1)} %copy-done.2, s32[1,16384]{1,0:T(1,128)S(1)} %bitcast.15, s32[1,8]{1,0:T(1,128)S(1)} %copy-done.16), custom_call_target="tpu_custom_call" | custom-call | tf_op jit(solution)/shard_map/pallas_call | solution.py:370
  (12 shorter events, 0.1 us)
Async XLA Ops:
  7.2 15.3 %copy-start = (f32[5,2048]{1,0:T(8,128)S(1)}, f32[5,2048]{1,0:T(8,128)}, u32[]{:S(2)}) copy-start(f32[5,2048]{1,0:T(8,128)} %param.21) | copy-start | bytes 122884
  7.2 37.8 %reduce-scatter.2.cloned.1.call-start = ((), (), s32[]{:S(2)}) async-start(), calls=%async_computation.2 | async-start | bytes 245760 | tf_op jit(solution)/shard_map/reduce_scatter | solution.py:350
  7.2 0.7 copy-start.16
  7.9 0.9 copy-start.1
  8.8 1.0 copy-start.3
  9.9 0.8 copy-start.5
  10.7 0.8 copy-start.7
  11.6 0.8 copy-start.9
  12.4 0.8 copy-start.11
  13.2 0.8 copy-start.13
  14.1 37.2 %copy-start.4 = (f32[5,16384]{1,0:T(8,128)S(1)}, f32[5,16384]{1,0:T(8,128)}, u32[]{:S(2)}) copy-start(f32[5,16384]{1,0:T(8,128)} %sp.3) | copy-start | bytes 983044
  14.1 37.2 %copy-start.10 = (s32[16384]{0:T(1024)S(1)}, s32[16384]{0:T(1024)}, u32[]{:S(2)}) copy-start(s32[16384]{0:T(1024)} %param.24) | copy-start | bytes 196612
  14.1 37.2 %copy-start.12 = (f32[16384]{0:T(1024)S(1)}, f32[16384]{0:T(1024)}, u32[]{:S(2)}) copy-start(f32[16384]{0:T(1024)} %param.17) | copy-start | bytes 196612
  14.1 37.2 %copy-start.14 = (s32[16384]{0:T(1024)S(1)}, s32[16384]{0:T(1024)}, u32[]{:S(2)}) copy-start(s32[16384]{0:T(1024)} %param.23) | copy-start | bytes 196612
  22.4 28.8 %copy-start.2 = (f32[3,16384]{1,0:T(4,128)S(1)}, f32[3,16384]{1,0:T(4,128)}, u32[]{:S(2)}) copy-start(f32[3,16384]{1,0:T(4,128)} %ad.5) | copy-start | bytes 589828
  22.5 28.8 %copy-start.6 = (f32[16384]{0:T(1024)S(1)}, f32[16384]{0:T(1024)}, u32[]{:S(2)}) copy-start(f32[16384]{0:T(1024)} %param.16) | copy-start | bytes 196612
  22.5 28.8 %copy-start.8 = (f32[16384]{0:T(1024)S(1)}, f32[16384]{0:T(1024)}, u32[]{:S(2)}) copy-start(f32[16384]{0:T(1024)} %param.18) | copy-start | bytes 196612
  45.0 0.8 copy-start.15
  71.0 0.7 copy-start.17
  72.0 4.3 %collective-permute-start.1 = (f32[32,128]{1,0:T(8,128)S(1)}, f32[32,128]{1,0:T(8,128)S(1)}, u32[]{:S(2)}, u32[]{:S(2)}) collective-permute-start(f32[32,128]{1,0:T(8,128)S(1)} %scatter-add.14.own), channel_id=1, source_target_pairs={{1,0},{2,1},{3,2},{4,3},{5,4},{6,5},{7,6},{8,7},{9,8},{10,9},{11,1... | collective-permute-start | bytes 49160 | tf_op jit(solution)/shard_map/ppermute | solution.py:365
  73.3 3.9 %collective-permute-start = (f32[32,128]{1,0:T(8,128)S(1)}, f32[32,128]{1,0:T(8,128)S(1)}, u32[]{:S(2)}, u32[]{:S(2)}) collective-permute-start(f32[32,128]{1,0:T(8,128)S(1)} %scatter-add.14.own), channel_id=1, source_target_pairs={{0,1},{1,2},{2,3},{3,4},{4,5},{5,6},{6,7},{7,8},{8,9},{9,10},{10,1... | collective-permute-start | bytes 49160 | tf_op jit(solution)/shard_map/ppermute | solution.py:364
Sparse Core Ops, SparseCore 0:
  22.5 22.4 reduce-scatter.1

commit v2 on v1

--- a/solution.py
+++ b/solution.py
@@ -199,13 +199,13 @@
     return [c / det for c in (c00, c01, c02, c11, c12, c22)]
 
 
-def window_of(before, own, after, halo, knots):
+def window_of(before, own, after, halo, knots, me, count):
     lane = lax.broadcasted_iota(jnp.int32, own.shape, 1)
     left = pltpu.roll(before, (halo - 1 - knots) % LANES, 1)
     right = pltpu.roll(after, (halo - 1 + knots) % LANES, 1)
     total = pltpu.roll(own, halo - 1, 1)
-    total = total + jnp.where(lane < halo + 2, left, 0.0)
-    return total + jnp.where(lane >= halo - 1 + knots, right, 0.0)
+    total = total + jnp.where((lane < halo + 2) & (me > 0), left, 0.0)
+    return total + jnp.where((lane >= halo - 1 + knots) & (me < count - 1), right, 0.0)
 
 
 def knot_valid(me, halo, knots, total):
@@ -240,136 +240,305 @@
     return pl.ds(pl.multiple_of(block * width, 128), width)
 
 
-def sums_kernel(knots, res, ow, tf, sp, ad, osrc, oint, cnt, out_sums, out_norm, acc):
-    blocks = cnt.shape[1]
-    width = res.shape[1] // blocks
-    groups = out_sums.shape[0]
+def pair_sum(received, blocks, first):
+    def step(number, total):
+        return total + received[first, number]
+
+    return lax.fori_loop(1, blocks, step, received[first, 0])
+
+
+def update_kernel(
+    n_src, n_seg, knots, halo,
+    res_in, ow_in, tf_in, sp_in, ad_in, osrc_in, oint_in, prior_in, att_in, cnt,
+    out_upd, out_att, out_res,
+    res, ow, tf, sp, ad, osrc, oint, prior, att_prior,
+    acc, sums, got_sums, upd, norm, got_norm, rhs, got_rhs, window, finals,
+    hot_lo, hot_knot, spline, corr,
+    in_sem, sum_send, sum_recv, upd_send, upd_recv, norm_send, norm_recv,
+    rhs_send, rhs_recv, fin_send, fin_recv,
+):
+    count = n_src * n_seg
+    src = lax.axis_index("src")
+    seg = lax.axis_index("seg")
+    me = src * n_seg + seg
+    width = res.shape[1] // n_src
+    groups = upd.shape[0]
+    share = groups // n_seg
+
+    loads = [
+        pltpu.make_async_copy(a, b, in_sem.at[number])
+        for number, (a, b) in enumerate(
+            [(osrc_in, osrc), (ow_in, ow), (sp_in, sp), (res_in, res), (oint_in, oint),
+             (tf_in, tf), (ad_in, ad), (att_in, att_prior), (prior_in, prior)]
+        )
+    ]
+    for load in loads:
+        load.start()
+
+    barrier = pltpu.get_barrier_semaphore()
+
+    def greet(number, carry):
+        other = lax.rem(me + number, count)
+        pl.semaphore_signal(
+            barrier, inc=1, device_id=(lax.div(other, n_seg), lax.rem(other, n_seg)),
+            device_id_type=pl.DeviceIdType.MESH,
+        )
+        return carry
+
+    lax.fori_loop(1, count, greet, 0)
+
+    def remote(a, b, send, recv, to_src, to_seg):
+        return pltpu.make_async_remote_copy(
+            src_ref=a, dst_ref=b, send_sem=send, recv_sem=recv,
+            device_id=(to_src, to_seg), device_id_type=pl.DeviceIdType.MESH,
+        )
+
     acc[...] = jnp.zeros_like(acc)
-
-    def step(block, carry):
+    for load in loads[:4]:
+        load.wait()
+
+    def source_step(block, carry):
+        sl = block_slice(block, width)
+        source = osrc[:, sl]
+        hot = one_hot(source % LO, LO)
+        hot_lo[block] = hot
+        weight = live_weight(ow[:, sl], cnt[0, block])
+        split = source_sums_block(sp[:, sl], weight, res[:, sl], source, hot)
+        acc[...] += contract_lanes(expand(split, source // LO, groups), hot)
+        return carry
+
+    lax.fori_loop(0, n_src, source_step, 0)
+    for group in range(groups):
+        sums[group] = acc[48 * group : 48 * group + 24] + acc[48 * group + 24 : 48 * group + 48]
+
+    pl.semaphore_wait(barrier, count - 1)
+
+    def sum_copy(step):
+        to = lax.rem(seg + step, n_seg)
+        return remote(sums.at[pl.ds(to * share, share)], got_sums.at[step - 1],
+                      sum_send.at[step - 1], sum_recv.at[step - 1], src, to)
+
+    for step in range(1, n_seg):
+        sum_copy(step).start()
+
+    for load in loads[4:]:
+        load.wait()
+
+    def knot_copy(buffer, got, send, recv, block, delta):
+        to = lax.rem(block * n_seg + seg + delta + count, count)
+        return remote(buffer.at[block], got.at[delta + 1, src], send.at[delta + 1, block],
+                      recv.at[delta + 1, src], lax.div(to, n_seg), lax.rem(to, n_seg))
+
+    def knot_send(buffer, got, send, recv, number, block):
+        knot_copy(buffer, got, send, recv, block, -1).start()
+        knot_copy(buffer, got, send, recv, block, 1).start()
+
+        @pl.when(number > 0)
+        def _():
+            knot_copy(buffer, got, send, recv, block, 0).start()
+
+        @pl.when(number == 0)
+        def _():
+            got[1, src] = buffer[src]
+
+    def knot_wait(buffer, got, send, recv):
+        def step(number, carry):
+            other = lax.rem(src + number, n_src)
+            for delta in (-1, 0, 1):
+                copy = remote(buffer.at[other], got.at[delta + 1, other],
+                              send.at[delta + 1, other], recv.at[delta + 1, other], src, seg)
+                if delta == 0:
+                    pl.when(number > 0)(copy.wait_recv)
+                else:
+                    copy.wait_recv()
+            return carry
+
+        lax.fori_loop(0, n_src, step, 0)
+
+    def knot_sent(buffer, got, send, recv):
+        def step(number, carry):
+            block = lax.rem(src + number, n_src)
+            for delta in (-1, 0, 1):
+                copy = knot_copy(buffer, got, send, recv, block, delta)
+                if delta == 0:
+                    pl.when(number > 0)(copy.wait_send)
+                else:
+                    copy.wait_send()
+            return carry
+
+        lax.fori_loop(0, n_src, step, 0)
+
+    norm_set = (norm, got_norm, norm_send, norm_recv)
+    rhs_set = (rhs, got_rhs, rhs_send, rhs_recv)
+
+    blank = jnp.zeros((3, LANES - knots), F32)
+    prior_ext = pltpu.roll(
+        jnp.concatenate(
+            [jnp.concatenate([att_prior[...], blank], 1), jnp.zeros((5, LANES), F32)], 0
+        ), 1, 1,
+    )
+    zero1 = jnp.zeros((1, LANES), F32)
+    zero2 = jnp.zeros((2, LANES), F32)
+    prior_rows = jnp.concatenate(
+        [prior_ext[0:1], zero2, prior_ext[1:2], zero1, prior_ext[2:3],
+         jnp.zeros((18, LANES), F32)], 0
+    )
+
+    def normal_step(number, carry):
+        block = lax.rem(src + number, n_src)
         sl = block_slice(block, width)
         weight = live_weight(ow[:, sl], cnt[0, block])
-        source = osrc[:, sl]
-        hot = one_hot(source % LO, LO)
-        split = source_sums_block(sp[:, sl], weight, res[:, sl], source, hot)
-        acc[...] += contract_lanes(expand(split, source // LO, groups), hot)
         floor_at, splines = basis(oint[:, sl], tf[:, sl], knots)
-        out_norm[block] = normal_block(ad[:, sl], weight, splines, one_hot(floor_at, LANES))
-        return carry
-
-    lax.fori_loop(0, blocks, step, 0)
-    for group in range(groups):
-        out_sums[group] = acc[48 * group : 48 * group + 24] + acc[48 * group + 24 : 48 * group + 48]
-
-
-def solve_kernel(sums, prior, out):
-    for group in range(sums.shape[0]):
-        out[group] = cholesky_solve5(sums[group], prior[:, group * LO : (group + 1) * LO])
-
-
-def first_kernel(knots, upd, res, ow, tf, sp, ad, osrc, oint, cnt, out_upd, out_corr, out_rhs):
-    blocks = cnt.shape[1]
-    width = res.shape[1] // blocks
-    groups = upd.shape[0]
+        hot = one_hot(floor_at, LANES)
+        hot_knot[block] = hot
+        spline[block] = jnp.concatenate(splines, 0)
+        first = jnp.where(number == 0, 1.0, 0.0)
+        norm[block] = normal_block(ad[:, sl], weight, splines, hot) + first * prior_rows
+        knot_send(*norm_set, number, block)
+        return carry
+
+    lax.fori_loop(0, n_src, normal_step, 0)
+
+    for step in range(1, n_seg):
+        sum_copy(step).wait_recv()
+    for group in range(share):
+        total = sums[seg * share + group]
+        for step in range(1, n_seg):
+            total = total + got_sums[step - 1, group]
+        start = pl.multiple_of((seg * share + group) * LO, LO)
+        upd[seg * share + group] = cholesky_solve5(total, prior[:, pl.ds(start, LO)])
+
+    def upd_copy(step, owner):
+        part = upd.at[pl.ds(owner * share, share)]
+        return remote(part, part, upd_send.at[step - 1], upd_recv.at[step - 1],
+                      src, lax.rem(seg + step, n_seg))
+
+    for step in range(1, n_seg):
+        upd_copy(step, seg).start()
+
+    knot_wait(*norm_set)
+    valid = knot_valid(me, halo, knots, count * knots)
+    normals = window_of(pair_sum(got_norm, n_src, 2), pair_sum(got_norm, n_src, 1),
+                        pair_sum(got_norm, n_src, 0), halo, knots, me, count)
+    diag, rows, inverse = prepare(normals, valid)
+    window[...] = jnp.concatenate(diag + rows[6:] + inverse + [zero2], 0)
+
+    for step in range(1, n_seg):
+        upd_copy(step, lax.rem(seg - step + n_seg, n_seg)).wait_recv()
     for group in range(groups):
         out_upd[:, group * LO : (group + 1) * LO] = upd[group, :5]
     table = split_rows(jnp.concatenate([upd[group] for group in range(groups)], 0))
 
-    def step(block, carry):
+    def first_step(number, carry):
+        block = lax.rem(src + number, n_src)
         sl = block_slice(block, width)
         weight = live_weight(ow[:, sl], cnt[0, block])
-        source = osrc[:, sl]
-        corr = source_lookup(table, one_hot(source % LO, LO), source // LO, sp[:, sl])
-        out_corr[:, sl] = corr
-        floor_at, splines = basis(oint[:, sl], tf[:, sl], knots)
-        out_rhs[block] = rhs_block(
-            ad[:, sl], weight * (res[:, sl] - corr), splines, one_hot(floor_at, LANES)
+        found = source_lookup(table, hot_lo[block], osrc[:, sl] // LO, sp[:, sl])
+        corr[:, sl] = found
+        splines = [spline[block, at : at + 1] for at in range(4)]
+        rhs[block] = rhs_block(
+            ad[:, sl], weight * (res[:, sl] - found), splines, hot_knot[block]
         )
-        return carry
-
-    lax.fori_loop(0, blocks, step, 0)
-
-
-def sweep_kernel(knots, total, halo, before, own, after, out_window, out_own):
-    me = lax.axis_index("src") * lax.axis_size("seg") + lax.axis_index("seg")
-    window = window_of(before[...], own[...], after[...], halo, knots)
-    valid = knot_valid(me, halo, knots, total)
-    diag, rows, inverse = prepare(window, valid)
-    rhs = [jnp.where(valid, window[24 + at : 25 + at], 0.0) for at in range(3)]
-    update = sweeps(diag, rows, inverse, rhs)
+        knot_send(*rhs_set, number, block)
+        return carry
+
+    lax.fori_loop(0, n_src, first_step, 0)
+
+    knot_wait(*rhs_set)
+    right = window_of(pair_sum(got_rhs, n_src, 2), pair_sum(got_rhs, n_src, 1),
+                      pair_sum(got_rhs, n_src, 0), halo, knots, me, count)
+    right = [jnp.where(valid, right[at : at + 1], 0.0) for at in range(3)]
+    rows = [window[at : at + 1] for at in range(24)]
+    inverse = [window[at : at + 1] for at in range(24, 30)]
+    update = sweeps(rows[:6], rows, inverse, right)
     final = jnp.concatenate(update + [jnp.zeros((5, LANES), F32)], 0)
-    out_window[...] = final
-    out_own[...] = pltpu.roll(final, LANES - halo, 1)[:3, :knots]
-
-
-def last_kernel(knots, halo, windows, corr, res, tf, ad, oint, cnt, out):
-    blocks = cnt.shape[1]
-    width = res.shape[1] // blocks
-
-    def step(block, carry):
+    finals[src] = final
+    out_att[...] = pltpu.roll(final, LANES - halo, 1)[:3, :knots]
+
+    def fin_copy(number, owner):
+        return remote(finals.at[owner], finals.at[owner], fin_send.at[number],
+                      fin_recv.at[number], lax.rem(src + number, n_src), seg)
+
+    def fin_start(number, carry):
+        fin_copy(number, src).start()
+        return carry
+
+    lax.fori_loop(1, n_src, fin_start, 0)
+
+    def last_step(number, carry):
+        block = lax.rem(src - number + n_src, n_src)
         sl = block_slice(block, width)
-        floor_at, splines = basis(oint[:, sl], tf[:, sl], knots)
-        att = attitude_lookup(
-            windows[block], halo - 1, one_hot(floor_at, LANES), splines, ad[:, sl]
-        )
-        residual = res[:, sl]
-        out[:, sl] = residual - live_weight(corr[:, sl] + att, cnt[0, block])
-        return carry
-
-    lax.fori_loop(0, blocks, step, 0)
-
-
-def call(kernel, outs, n_vmem, count=False, scratch=()):
-    return pl.pallas_call(
-        kernel,
-        out_shape=[jax.ShapeDtypeStruct(shape, F32) for shape in outs],
-        in_specs=[vmem] * n_vmem + [smem] * count,
-        out_specs=[vmem] * len(outs),
-        scratch_shapes=list(scratch),
-        compiler_params=pltpu.CompilerParams(vmem_limit_bytes=40 * 2**20),
-    )
+
+        @pl.when(number > 0)
+        def _():
+            fin_copy(number, block).wait_recv()
+
+        splines = [spline[block, at : at + 1] for at in range(4)]
+        att = attitude_lookup(finals[block], halo - 1, hot_knot[block], splines, ad[:, sl])
+        out_res[:, sl] = res[:, sl] - live_weight(corr[:, sl] + att, cnt[0, block])
+        return carry
+
+    lax.fori_loop(0, n_src, last_step, 0)
+
+    def fin_sent(number, carry):
+        fin_copy(number, src).wait_send()
+        return carry
+
+    lax.fori_loop(1, n_src, fin_sent, 0)
+    for step in range(1, n_seg):
+        sum_copy(step).wait_send()
+        upd_copy(step, seg).wait_send()
+    knot_sent(*norm_set)
+    knot_sent(*rhs_set)
 
 
 def body(residual, obs_weight, time_frac, src_partials, att_dir, src_prior, att_prior,
          obs_source, obs_interval, obs_count):
     n_src = lax.axis_size("src")
     n_seg = lax.axis_size("seg")
-    seg_at = lax.axis_index("seg")
     obs = residual.shape[0]
     sources = src_prior.shape[1]
     knots = att_prior.shape[1]
-    total = knots * n_src * n_seg
     groups = sources // LO
-    halo = 32
-    rows = [x.reshape(1, obs) for x in (residual, obs_weight, time_frac, obs_source, obs_interval)]
-    res, ow, tf, osrc, oint = rows
-    sums, normals = call(
-        functools.partial(sums_kernel, knots),
-        [(groups, 24, LO), (n_src, 24, LANES)], 7, True, [pltpu.VMEM((groups * 48, LO), F32)],
-    )(res, ow, tf, src_partials, att_dir, osrc, oint, obs_count)
-    part = lax.psum_scatter(sums, "seg", scatter_dimension=0, tiled=True)
-    share = sources // n_seg
-    prior = lax.dynamic_slice_in_dim(src_prior, seg_at * share, share, 1)
-    (upd,) = call(solve_kernel, [(groups // n_seg, 8, LO)], 2)(part, prior)
-    upd = lax.all_gather(upd, "seg", axis=0, tiled=True)
-    src_update, corr, rhs = call(
-        functools.partial(first_kernel, knots),
-        [(5, sources), (1, obs), (n_src, 8, LANES)], 8, True,
-    )(upd, res, ow, tf, src_partials, att_dir, osrc, oint, obs_count)
-    sent = jnp.concatenate([normals, rhs], 1)
-    own = jnp.sum(lax.all_to_all(sent, "src", split_axis=0, concat_axis=0, tiled=True), 0)
-    prior_ext = jnp.pad(att_prior, ((0, 0), (1, LANES - 1 - knots)))
-    own = own.at[0].add(prior_ext[0]).at[3].add(prior_ext[1]).at[5].add(prior_ext[2])
-    count = n_src * n_seg
-    before = lax.ppermute(own, ("src", "seg"), [(i, i + 1) for i in range(count - 1)])
-    after = lax.ppermute(own, ("src", "seg"), [(i + 1, i) for i in range(count - 1)])
-    window, att_update = call(
-        functools.partial(sweep_kernel, knots, total, halo), [(8, LANES), (3, knots)], 3
-    )(before, own, after)
-    windows = lax.all_gather(window, "src", axis=0)
-    (out,) = call(functools.partial(last_kernel, knots, halo), [(1, obs)], 6, True)(
-        windows, corr, res, tf, att_dir, oint, obs_count
-    )
+    share = groups // n_seg
+    width = obs // n_src
+    row = lambda x: x.reshape(1, obs)
+    ints = pltpu.VMEM((1, obs), jnp.int32)
+    line = pltpu.VMEM((1, obs), F32)
+    dma = pltpu.SemaphoreType.DMA
+    anywhere = pl.BlockSpec(memory_space=pl.ANY)
+    src_update, att_update, out = pl.pallas_call(
+        functools.partial(update_kernel, n_src, n_seg, knots, 32),
+        out_shape=[jax.ShapeDtypeStruct(shape, F32)
+                   for shape in ((5, sources), (3, knots), (1, obs))],
+        in_specs=[anywhere] * 9 + [smem],
+        out_specs=[vmem] * 3,
+        scratch_shapes=[
+            line, line, line, pltpu.VMEM((5, obs), F32), pltpu.VMEM((3, obs), F32), ints, ints,
+            pltpu.VMEM((5, sources), F32), pltpu.VMEM((3, knots), F32),
+            pltpu.VMEM((groups * 48, LO), F32),
+            pltpu.VMEM((groups, 24, LO), F32),
+            pltpu.VMEM((n_seg - 1, share, 24, LO), F32),
+            pltpu.VMEM((groups, 8, LO), F32),
+            pltpu.VMEM((n_src, 24, LANES), F32),
+            pltpu.VMEM((3, n_src, 24, LANES), F32),
+            pltpu.VMEM((n_src, 8, LANES), F32),
+            pltpu.VMEM((3, n_src, 8, LANES), F32),
+            pltpu.VMEM((32, LANES), F32),
+            pltpu.VMEM((n_src, 8, LANES), F32),
+            pltpu.VMEM((n_src, LO, width), BF16),
+            pltpu.VMEM((n_src, LANES, width), BF16),
+            pltpu.VMEM((n_src, 4, width), F32),
+            line,
+            dma((9,)), dma((n_seg - 1,)), dma((n_seg - 1,)), dma((n_seg - 1,)), dma((n_seg - 1,)),
+            dma((3, n_src)), dma((3, n_src)), dma((3, n_src)), dma((3, n_src)),
+            dma((n_src,)), dma((n_src,)),
+        ],
+        compiler_params=pltpu.CompilerParams(
+            collective_id=0, has_side_effects=True, vmem_limit_bytes=56 * 2**20
+        ),
+    )(row(residual), row(obs_weight), row(time_frac), src_partials, att_dir, row(obs_source),
+      row(obs_interval), src_prior, att_prior, obs_count)
     return src_update, att_update, out.reshape(obs)
 
 

time: 121 us -> 42.3 us (0.35)
  blocking collectives: 49.4 us -> 0 us
  waiting for transfers between devices: 23.4 us -> 0 us
  Pallas kernels: 20.7 us -> 38.7 us
  between operations: 14.2 us -> 0.66 us
  local copies, waits for them, and re-layouts: 8.42 us -> 2.73 us
  starting transfers between devices: 4.35 us -> 0 us
    all_gather x2 -> x0, blocking collectives: 36.5 us -> none  [the longest x1 31.3 us: body(): windows = lax.all_gather(window, 'src', axis=0)]
    reduce_scatter x1 -> x0, waiting for transfers between devices: 22.5 us -> none  [body(): part = lax.psum_scatter(sums, 'seg', scatter_dimension=0, tiled=True)]
    pallas_call x5 -> x1, Pallas kernels: 20.7 us -> 38.7 us  [body(): pl.pallas_call(functools.partial(update_kernel, n_src, n_seg, knots, 32),...]
    all_to_all x1 -> x0, blocking collectives: 12.8 us -> none  [body(): lax.all_to_all(sent, 'src', split_axis=0, concat_axis=0, tiled=True)]
    unnamed x36 -> x7, local copies, waits for them, and re-layouts: 8.34 us -> 2.73 us
    ppermute x2 -> x0, starting transfers between devices: 4.31 us -> none  [the longest x1 3.03 us: body(): lax.ppermute(own, ('src', 'seg'), [(i, i + 1) for i in range(count - 1)])]
  transfers between devices with their start and end apart: 3 -> 0, of which waited for: 2 -> 0; matrix products, arithmetic and copies ran while one was open for 0% -> 0% of each run, Pallas kernels for 0% -> 0%
where the time goes in v2:
time: 42.3 us; the launch traced here: 42.1 us
  Pallas kernels  38.7 us (91%)
  local copies, waits for them, and re-layouts  2.73 us (6%)
  between operations  0.66 us (2%)
    pallas_call x1, Pallas kernels, body(): pl.pallas_call(functools.partial(update_kernel, n_src, n_seg, knots, 32),...  38.7 us
    unnamed x7, local copies, waits for them, and re-layouts  2.73 us

profile of v2, /device:TPU:0, one launch (start us, length us, event | category | flops | bytes accessed | tf_op | source)
XLA Modules:
  0.0 42.1 jit_solution(4114197644490240903)
XLA Ops:
  0.6 38.7 %shard_map.121 = (f32[5,2048]{1,0:T(8,128)}, f32[3,64]{1,0:T(4,128)}, f32[1,16384]{1,0:T(1,128)}) custom-call(f32[1,16384]{1,0:T(1,128)} %bitcast.6, f32[1,16384]{1,0:T(1,128)} %bitcast.7, f32[1,16384]{1,0:T(1,128)} %bitcast.8, f32[5,16384]{1,0:T(8,128)} %sp_in.1, f32[3,16384]{1,0:T(4,128)} %ad_in.1, s32[1,16384]{1,0:T(1,128)} %bitcast.9, ...), custom_call_target="tpu_custom_call" | custom-call | tf_op jit(solution)/shard_map/pallas_call | solution.py:510
  39.4 0.0 copy-start.1
  39.4 0.0 copy-start
  39.4 1.5 %copy.16 = f32[5,2048]{1,0:T(8,128)} copy(f32[5,2048]{1,0:T(8,128)} %get-tuple-element.12) | data formatting | bytes 81920
  40.9 0.0 copy-done.1
  40.9 0.6 %copy.17 = f32[3,64]{1,0:T(4,128)} copy(f32[3,64]{1,0:T(4,128)S(1)} %copy-done.1) | data formatting | bytes 1536
  41.5 0.0 copy-done
  41.5 0.6 %copy.18 = f32[16384]{0:T(1024)} copy(f32[16384]{0:T(1024)S(1)} %bitcast.11) | data formatting | bytes 131072
Async XLA Ops:
  39.4 1.5 %copy-start.1 = (f32[3,64]{1,0:T(4,128)S(1)}, f32[3,64]{1,0:T(4,128)}, u32[]{:S(2)}) copy-start(f32[3,64]{1,0:T(4,128)} %get-tuple-element.13) | copy-start | bytes 2308
  39.4 2.1 %copy-start = (f32[1,16384]{1,0:T(1,128)S(1)}, f32[1,16384]{1,0:T(1,128)}, u32[]{:S(2)}) copy-start(f32[1,16384]{1,0:T(1,128)} %get-tuple-element.8) | copy-start | bytes 196612

commit v3 on v2

--- a/solution.py
+++ b/solution.py
@@ -9,6 +9,8 @@
 
 ITERS_ATT = 6
 LO = 256
+LO_BITS = 8
+SIXTH = 1.0 / 6.0
 LANES = 128
 F32 = jnp.float32
 BF16 = jnp.bfloat16
@@ -37,8 +39,14 @@
 
 
 def one_hot(index_row, rows):
-    ids = lax.broadcasted_iota(jnp.int32, (rows, index_row.shape[1]), 0)
-    return jnp.where(ids == index_row, 1.0, 0.0).astype(BF16)
+    width = index_row.shape[1]
+    ids = lax.broadcasted_iota(jnp.int32, (16, width), 0).astype(F32).astype(BF16)
+    wanted = jnp.broadcast_to(index_row.astype(F32), (16, width)).astype(BF16)
+    one = jnp.ones((16, width), BF16)
+    zero = jnp.zeros((16, width), BF16)
+    return jnp.concatenate(
+        [jnp.where(wanted == ids + start, one, zero) for start in range(0, rows, 16)], 0
+    )
 
 
 def live_weight(weight_row, count):
@@ -46,18 +54,18 @@
     return jnp.where(place < count, weight_row, 0.0)
 
 
-def basis(interval_row, frac_row, knots):
-    local_time = (interval_row % knots).astype(F32) + frac_row
+def basis(interval_row, frac_row, first):
+    local_time = (interval_row - first).astype(F32) + frac_row
     floor_part = jnp.floor(local_time)
     u = local_time - floor_part
     square = u * u
     cube = square * u
     rest = 1.0 - u
     splines = [
-        rest * rest * rest / 6.0,
-        (3.0 * cube - 6.0 * square + 4.0) / 6.0,
-        (-3.0 * cube + 3.0 * square + 3.0 * u + 1.0) / 6.0,
-        cube / 6.0,
+        rest * rest * rest * SIXTH,
+        (3.0 * cube - 6.0 * square + 4.0) * SIXTH,
+        (-3.0 * cube + 3.0 * square + 3.0 * u + 1.0) * SIXTH,
+        cube * SIXTH,
     ]
     return floor_part.astype(jnp.int32), splines
 
@@ -129,6 +137,7 @@
 
 def cholesky_solve5(sums, prior):
     factor = {}
+    inverse = [None] * 5
     for row in range(5):
         for col in range(row + 1):
             at = PAIR_ROW[row, col]
@@ -138,21 +147,21 @@
             for k in range(col):
                 running = running - factor[row, k] * factor[col, k]
             if row == col:
-                factor[row, row] = jnp.sqrt(running)
+                inverse[row] = 1.0 / jnp.sqrt(running)
             else:
-                factor[row, col] = running / factor[col, col]
+                factor[row, col] = running * inverse[col]
     forward = []
     for row in range(5):
         running = sums[15 + row : 16 + row]
         for k in range(row):
             running = running - factor[row, k] * forward[k]
-        forward.append(running / factor[row, row])
+        forward.append(running * inverse[row])
     backward = [None] * 5
     for row in reversed(range(5)):
         running = forward[row]
         for k in range(row + 1, 5):
             running = running - factor[k, row] * backward[k]
-        backward[row] = running / factor[row, row]
+        backward[row] = running * inverse[row]
     return jnp.concatenate(backward + [jnp.zeros((3, LO), F32)], 0)
 
 
@@ -252,9 +261,9 @@
     res_in, ow_in, tf_in, sp_in, ad_in, osrc_in, oint_in, prior_in, att_in, cnt,
     out_upd, out_att, out_res,
     res, ow, tf, sp, ad, osrc, oint, prior, att_prior,
-    acc, sums, got_sums, upd, norm, got_norm, rhs, got_rhs, window, finals,
+    acc, sums, got_sums, upd, norm, got_norm, own_norm, beside, rhs, got_rhs, finals,
     hot_lo, hot_knot, spline, corr,
-    in_sem, sum_send, sum_recv, upd_send, upd_recv, norm_send, norm_recv,
+    in_sem, sum_send, sum_recv, upd_send, upd_recv, norm_send, norm_recv, beside_send, beside_recv,
     rhs_send, rhs_recv, fin_send, fin_recv,
 ):
     count = n_src * n_seg
@@ -300,11 +309,11 @@
     def source_step(block, carry):
         sl = block_slice(block, width)
         source = osrc[:, sl]
-        hot = one_hot(source % LO, LO)
+        hot = one_hot(source & (LO - 1), LO)
         hot_lo[block] = hot
         weight = live_weight(ow[:, sl], cnt[0, block])
         split = source_sums_block(sp[:, sl], weight, res[:, sl], source, hot)
-        acc[...] += contract_lanes(expand(split, source // LO, groups), hot)
+        acc[...] += contract_lanes(expand(split, source >> LO_BITS, groups), hot)
         return carry
 
     lax.fori_loop(0, n_src, source_step, 0)
@@ -368,7 +377,15 @@
 
         lax.fori_loop(0, n_src, step, 0)
 
-    norm_set = (norm, got_norm, norm_send, norm_recv)
+    def norm_copy(number, block):
+        return remote(norm.at[block], got_norm.at[number - 1], norm_send.at[number - 1],
+                      norm_recv.at[number - 1], block, seg)
+
+    def beside_copy(slot):
+        to = lax.rem(me + (1 if slot == 0 else count - 1), count)
+        return remote(own_norm, beside.at[slot], beside_send.at[slot], beside_recv.at[slot],
+                      lax.div(to, n_seg), lax.rem(to, n_seg))
+
     rhs_set = (rhs, got_rhs, rhs_send, rhs_recv)
 
     blank = jnp.zeros((3, LANES - knots), F32)
@@ -388,13 +405,16 @@
         block = lax.rem(src + number, n_src)
         sl = block_slice(block, width)
         weight = live_weight(ow[:, sl], cnt[0, block])
-        floor_at, splines = basis(oint[:, sl], tf[:, sl], knots)
+        floor_at, splines = basis(oint[:, sl], tf[:, sl], (block * n_seg + seg) * knots)
         hot = one_hot(floor_at, LANES)
         hot_knot[block] = hot
         spline[block] = jnp.concatenate(splines, 0)
-        first = jnp.where(number == 0, 1.0, 0.0)
-        norm[block] = normal_block(ad[:, sl], weight, splines, hot) + first * prior_rows
-        knot_send(*norm_set, number, block)
+        norm[block] = normal_block(ad[:, sl], weight, splines, hot)
+
+        @pl.when(number > 0)
+        def _():
+            norm_copy(number, block).start()
+
         return carry
 
     lax.fori_loop(0, n_src, normal_step, 0)
@@ -416,12 +436,13 @@
     for step in range(1, n_seg):
         upd_copy(step, seg).start()
 
-    knot_wait(*norm_set)
-    valid = knot_valid(me, halo, knots, count * knots)
-    normals = window_of(pair_sum(got_norm, n_src, 2), pair_sum(got_norm, n_src, 1),
-                        pair_sum(got_norm, n_src, 0), halo, knots, me, count)
-    diag, rows, inverse = prepare(normals, valid)
-    window[...] = jnp.concatenate(diag + rows[6:] + inverse + [zero2], 0)
+    def norm_sum(number, total):
+        norm_copy(number, src).wait_recv()
+        return total + got_norm[number - 1]
+
+    own_norm[...] = lax.fori_loop(1, n_src, norm_sum, norm[src] + prior_rows)
+    for slot in range(2):
+        beside_copy(slot).start()
 
     for step in range(1, n_seg):
         upd_copy(step, lax.rem(seg - step + n_seg, n_seg)).wait_recv()
@@ -433,7 +454,7 @@
         block = lax.rem(src + number, n_src)
         sl = block_slice(block, width)
         weight = live_weight(ow[:, sl], cnt[0, block])
-        found = source_lookup(table, hot_lo[block], osrc[:, sl] // LO, sp[:, sl])
+        found = source_lookup(table, hot_lo[block], osrc[:, sl] >> LO_BITS, sp[:, sl])
         corr[:, sl] = found
         splines = [spline[block, at : at + 1] for at in range(4)]
         rhs[block] = rhs_block(
@@ -444,13 +465,17 @@
 
     lax.fori_loop(0, n_src, first_step, 0)
 
+    for slot in range(2):
+        beside_copy(slot).wait_recv()
+    valid = knot_valid(me, halo, knots, count * knots)
+    normals = window_of(beside[0], own_norm[...], beside[1], halo, knots, me, count)
+    diag, rows, inverse = prepare(normals, valid)
+
     knot_wait(*rhs_set)
     right = window_of(pair_sum(got_rhs, n_src, 2), pair_sum(got_rhs, n_src, 1),
                       pair_sum(got_rhs, n_src, 0), halo, knots, me, count)
     right = [jnp.where(valid, right[at : at + 1], 0.0) for at in range(3)]
-    rows = [window[at : at + 1] for at in range(24)]
-    inverse = [window[at : at + 1] for at in range(24, 30)]
-    update = sweeps(rows[:6], rows, inverse, right)
+    update = sweeps(diag, rows, inverse, right)
     final = jnp.concatenate(update + [jnp.zeros((5, LANES), F32)], 0)
     finals[src] = final
     out_att[...] = pltpu.roll(final, LANES - halo, 1)[:3, :knots]
@@ -488,7 +513,14 @@
     for step in range(1, n_seg):
         sum_copy(step).wait_send()
         upd_copy(step, seg).wait_send()
-    knot_sent(*norm_set)
+    for slot in range(2):
+        beside_copy(slot).wait_send()
+
+    def norm_sent(number, carry):
+        norm_copy(number, lax.rem(src + number, n_src)).wait_send()
+        return carry
+
+    lax.fori_loop(1, n_src, norm_sent, 0)
     knot_sent(*rhs_set)
 
 
@@ -521,17 +553,19 @@
             pltpu.VMEM((n_seg - 1, share, 24, LO), F32),
             pltpu.VMEM((groups, 8, LO), F32),
             pltpu.VMEM((n_src, 24, LANES), F32),
-            pltpu.VMEM((3, n_src, 24, LANES), F32),
+            pltpu.VMEM((n_src - 1, 24, LANES), F32),
+            pltpu.VMEM((24, LANES), F32),
+            pltpu.VMEM((2, 24, LANES), F32),
             pltpu.VMEM((n_src, 8, LANES), F32),
             pltpu.VMEM((3, n_src, 8, LANES), F32),
-            pltpu.VMEM((32, LANES), F32),
             pltpu.VMEM((n_src, 8, LANES), F32),
             pltpu.VMEM((n_src, LO, width), BF16),
             pltpu.VMEM((n_src, LANES, width), BF16),
             pltpu.VMEM((n_src, 4, width), F32),
             line,
             dma((9,)), dma((n_seg - 1,)), dma((n_seg - 1,)), dma((n_seg - 1,)), dma((n_seg - 1,)),
-            dma((3, n_src)), dma((3, n_src)), dma((3, n_src)), dma((3, n_src)),
+            dma((n_src - 1,)), dma((n_src - 1,)), dma((2,)), dma((2,)),
+            dma((3, n_src)), dma((3, n_src)),
             dma((n_src,)), dma((n_src,)),
         ],
         compiler_params=pltpu.CompilerParams(

time: 42.3 us -> 38.1 us (0.901)
  Pallas kernels: 38.7 us -> 34.5 us
    pallas_call x1, Pallas kernels: 38.7 us -> 34.5 us  [body(): pl.pallas_call(functools.partial(update_kernel, n_src, n_seg, knots, 32),...]
where the time goes in v3:
time: 38.1 us; the launch traced here: 37.9 us
  Pallas kernels  34.5 us (91%)
  local copies, waits for them, and re-layouts  2.73 us (7%)
  between operations  0.66 us (2%)
    pallas_call x1, Pallas kernels, body(): pl.pallas_call(functools.partial(update_kernel, n_src, n_seg, knots, 32),...  34.5 us
    unnamed x7, local copies, waits for them, and re-layouts  2.73 us

profile of v3, /device:TPU:0, one launch (start us, length us, event | category | flops | bytes accessed | tf_op | source)
XLA Modules:
  0.0 37.9 jit_solution(3278410297680380958)
XLA Ops:
  0.6 34.5 %shard_map.121 = (f32[5,2048]{1,0:T(8,128)}, f32[3,64]{1,0:T(4,128)}, f32[1,16384]{1,0:T(1,128)}) custom-call(f32[1,16384]{1,0:T(1,128)} %bitcast.6, f32[1,16384]{1,0:T(1,128)} %bitcast.7, f32[1,16384]{1,0:T(1,128)} %bitcast.8, f32[5,16384]{1,0:T(8,128)} %sp_in.1, f32[3,16384]{1,0:T(4,128)} %ad_in.1, s32[1,16384]{1,0:T(1,128)} %bitcast.9, ...), custom_call_target="tpu_custom_call" | custom-call | tf_op jit(solution)/shard_map/pallas_call | solution.py:542
  35.2 0.0 copy-start.1
  35.2 0.0 copy-start
  35.2 1.5 %copy.16 = f32[5,2048]{1,0:T(8,128)} copy(f32[5,2048]{1,0:T(8,128)} %get-tuple-element.12) | data formatting | bytes 81920
  36.7 0.0 copy-done.1
  36.7 0.6 %copy.17 = f32[3,64]{1,0:T(4,128)} copy(f32[3,64]{1,0:T(4,128)S(1)} %copy-done.1) | data formatting | bytes 1536
  37.3 0.0 copy-done
  37.3 0.6 %copy.18 = f32[16384]{0:T(1024)} copy(f32[16384]{0:T(1024)S(1)} %bitcast.11) | data formatting | bytes 131072
Async XLA Ops:
  35.2 1.5 %copy-start.1 = (f32[3,64]{1,0:T(4,128)S(1)}, f32[3,64]{1,0:T(4,128)}, u32[]{:S(2)}) copy-start(f32[3,64]{1,0:T(4,128)} %get-tuple-element.13) | copy-start | bytes 2308
  35.2 2.1 %copy-start = (f32[1,16384]{1,0:T(1,128)S(1)}, f32[1,16384]{1,0:T(1,128)}, u32[]{:S(2)}) copy-start(f32[1,16384]{1,0:T(1,128)} %get-tuple-element.8) | copy-start | bytes 196612

commit v4 on v3

--- a/solution.py
+++ b/solution.py
@@ -88,12 +88,13 @@
 
 def expand(split, high_row, groups):
     width = split.shape[1]
-    high16 = jnp.broadcast_to(high_row, (16, width))
+    high16 = jnp.broadcast_to(high_row.astype(F32), (16, width)).astype(BF16)
+    zero = jnp.zeros((16, width), BF16)
     parts = []
     for group in range(groups):
-        mask = jnp.where(high16 == group, 1.0, 0.0).astype(BF16)
+        mask = high16 == jnp.full((16, width), group, BF16)
         for start in range(0, split.shape[0], 16):
-            parts.append(split[start : start + 16] * mask)
+            parts.append(jnp.where(mask, split[start : start + 16], zero))
     return jnp.concatenate(parts, 0)
 
 
@@ -230,16 +231,23 @@
     return diag, rows, inverse
 
 
-def sweeps(diag, rows, inverse, rhs):
+def shift_back(rows):
+    return [
+        pltpu.roll(rows[6 * offset + at], offset, 1) for offset in range(1, 4) for at in range(6)
+    ]
+
+
+def sweeps(diag, rows, lower, inverse, rhs):
     update = [damping * x for x in sym_apply(inverse, rhs)]
     for _ in range(1, ITERS_ATT):
         applied = sym_apply(diag, update)
         for offset in range(1, 4):
-            upper = rows[6 * offset : 6 * offset + 6]
             ahead = [pltpu.roll(x, LANES - offset, 1) for x in update]
-            behind = [pltpu.roll(x, offset, 1) for x in sym_apply(upper, update)]
-            for at, x in enumerate(sym_apply(upper, ahead)):
-                applied[at] = applied[at] + x + behind[at]
+            behind = [pltpu.roll(x, offset, 1) for x in update]
+            upper_part = sym_apply(rows[6 * offset : 6 * offset + 6], ahead)
+            lower_part = sym_apply(lower[6 * offset - 6 : 6 * offset], behind)
+            for at in range(3):
+                applied[at] = applied[at] + (upper_part[at] + lower_part[at])
         step = sym_apply(inverse, [rhs[at] - applied[at] for at in range(3)])
         update = [update[at] + damping * step[at] for at in range(3)]
     return update
@@ -259,11 +267,12 @@
 def update_kernel(
     n_src, n_seg, knots, halo,
     res_in, ow_in, tf_in, sp_in, ad_in, osrc_in, oint_in, prior_in, att_in, cnt,
+    upd_to, att_to, res_to,
     out_upd, out_att, out_res,
     res, ow, tf, sp, ad, osrc, oint, prior, att_prior,
     acc, sums, got_sums, upd, norm, got_norm, own_norm, beside, rhs, got_rhs, finals,
     hot_lo, hot_knot, spline, corr,
-    in_sem, sum_send, sum_recv, upd_send, upd_recv, norm_send, norm_recv, beside_send, beside_recv,
+    in_sem, out_sem, res_sem, sum_send, sum_recv, upd_send, upd_recv, norm_send, norm_recv, beside_send, beside_recv,
     rhs_send, rhs_recv, fin_send, fin_recv,
 ):
     count = n_src * n_seg
@@ -448,6 +457,8 @@
         upd_copy(step, lax.rem(seg - step + n_seg, n_seg)).wait_recv()
     for group in range(groups):
         out_upd[:, group * LO : (group + 1) * LO] = upd[group, :5]
+    upd_store = pltpu.make_async_copy(out_upd, upd_to, out_sem.at[0])
+    upd_store.start()
     table = split_rows(jnp.concatenate([upd[group] for group in range(groups)], 0))
 
     def first_step(number, carry):
@@ -459,7 +470,7 @@
         splines = [spline[block, at : at + 1] for at in range(4)]
         rhs[block] = rhs_block(
             ad[:, sl], weight * (res[:, sl] - found), splines, hot_knot[block]
-        )
+        )[:4]
         knot_send(*rhs_set, number, block)
         return carry
 
@@ -470,15 +481,15 @@
     valid = knot_valid(me, halo, knots, count * knots)
     normals = window_of(beside[0], own_norm[...], beside[1], halo, knots, me, count)
     diag, rows, inverse = prepare(normals, valid)
+    lower = shift_back(rows)
 
     knot_wait(*rhs_set)
     right = window_of(pair_sum(got_rhs, n_src, 2), pair_sum(got_rhs, n_src, 1),
                       pair_sum(got_rhs, n_src, 0), halo, knots, me, count)
     right = [jnp.where(valid, right[at : at + 1], 0.0) for at in range(3)]
-    update = sweeps(diag, rows, inverse, right)
+    update = sweeps(diag, rows, lower, inverse, right)
     final = jnp.concatenate(update + [jnp.zeros((5, LANES), F32)], 0)
     finals[src] = final
-    out_att[...] = pltpu.roll(final, LANES - halo, 1)[:3, :knots]
 
     def fin_copy(number, owner):
         return remote(finals.at[owner], finals.at[owner], fin_send.at[number],
@@ -490,6 +501,14 @@
 
     lax.fori_loop(1, n_src, fin_start, 0)
 
+    out_att[...] = pltpu.roll(final, LANES - halo, 1)[:3, :knots]
+    att_store = pltpu.make_async_copy(out_att, att_to, out_sem.at[1])
+    att_store.start()
+
+    def res_store(number, block):
+        sl = block_slice(block, width)
+        return pltpu.make_async_copy(out_res.at[:, sl], res_to.at[:, sl], res_sem.at[number])
+
     def last_step(number, carry):
         block = lax.rem(src - number + n_src, n_src)
         sl = block_slice(block, width)
@@ -501,6 +520,7 @@
         splines = [spline[block, at : at + 1] for at in range(4)]
         att = attitude_lookup(finals[block], halo - 1, hot_knot[block], splines, ad[:, sl])
         out_res[:, sl] = res[:, sl] - live_weight(corr[:, sl] + att, cnt[0, block])
+        res_store(number, block).start()
         return carry
 
     lax.fori_loop(0, n_src, last_step, 0)
@@ -522,6 +542,25 @@
 
     lax.fori_loop(1, n_src, norm_sent, 0)
     knot_sent(*rhs_set)
+    upd_store.wait()
+    att_store.wait()
+
+    def res_stored(number, carry):
+        res_store(number, lax.rem(src - number + n_src, n_src)).wait()
+        return carry
+
+    lax.fori_loop(0, n_src, res_stored, 0)
+
+
+def hand_over(a, b, c, a_to, b_to, c_to, sem):
+    copies = [
+        pltpu.make_async_copy(x, y, sem.at[number])
+        for number, (x, y) in enumerate([(c, c_to), (a, a_to), (b, b_to)])
+    ]
+    for copy in copies:
+        copy.start()
+    for copy in copies:
+        copy.wait()
 
 
 def body(residual, obs_weight, time_frac, src_partials, att_dir, src_prior, att_prior,
@@ -539,13 +578,14 @@
     line = pltpu.VMEM((1, obs), F32)
     dma = pltpu.SemaphoreType.DMA
     anywhere = pl.BlockSpec(memory_space=pl.ANY)
-    src_update, att_update, out = pl.pallas_call(
+    outs = [jax.ShapeDtypeStruct(shape, F32) for shape in ((5, sources), (3, knots), (1, obs))]
+    made = pl.pallas_call(
         functools.partial(update_kernel, n_src, n_seg, knots, 32),
-        out_shape=[jax.ShapeDtypeStruct(shape, F32)
-                   for shape in ((5, sources), (3, knots), (1, obs))],
+        out_shape=outs,
         in_specs=[anywhere] * 9 + [smem],
-        out_specs=[vmem] * 3,
+        out_specs=[anywhere] * 3,
         scratch_shapes=[
+            pltpu.VMEM((5, sources), F32), pltpu.VMEM((3, knots), F32), line,
             line, line, line, pltpu.VMEM((5, obs), F32), pltpu.VMEM((3, obs), F32), ints, ints,
             pltpu.VMEM((5, sources), F32), pltpu.VMEM((3, knots), F32),
             pltpu.VMEM((groups * 48, LO), F32),
@@ -556,14 +596,14 @@
             pltpu.VMEM((n_src - 1, 24, LANES), F32),
             pltpu.VMEM((24, LANES), F32),
             pltpu.VMEM((2, 24, LANES), F32),
-            pltpu.VMEM((n_src, 8, LANES), F32),
-            pltpu.VMEM((3, n_src, 8, LANES), F32),
+            pltpu.VMEM((n_src, 4, LANES), F32),
+            pltpu.VMEM((3, n_src, 4, LANES), F32),
             pltpu.VMEM((n_src, 8, LANES), F32),
             pltpu.VMEM((n_src, LO, width), BF16),
             pltpu.VMEM((n_src, LANES, width), BF16),
             pltpu.VMEM((n_src, 4, width), F32),
             line,
-            dma((9,)), dma((n_seg - 1,)), dma((n_seg - 1,)), dma((n_seg - 1,)), dma((n_seg - 1,)),
+            dma((9,)), dma((2,)), dma((n_src,)), dma((n_seg - 1,)), dma((n_seg - 1,)), dma((n_seg - 1,)), dma((n_seg - 1,)),
             dma((n_src - 1,)), dma((n_src - 1,)), dma((2,)), dma((2,)),
             dma((3, n_src)), dma((3, n_src)),
             dma((n_src,)), dma((n_src,)),
@@ -573,6 +613,14 @@
         ),
     )(row(residual), row(obs_weight), row(time_frac), src_partials, att_dir, row(obs_source),
       row(obs_interval), src_prior, att_prior, obs_count)
+    src_update, att_update, out = pl.pallas_call(
+        hand_over,
+        out_shape=outs,
+        in_specs=[anywhere] * 3,
+        out_specs=[anywhere] * 3,
+        scratch_shapes=[dma((3,))],
+        compiler_params=pltpu.CompilerParams(vmem_limit_bytes=56 * 2**20),
+    )(*made)
     return src_update, att_update, out.reshape(obs)
 
 

time: 38.1 us -> 40.2 us (1.055)
  Pallas kernels: 34.5 us -> 39.4 us
  local copies, waits for them, and re-layouts: 2.73 us -> 0 us
    pallas_call x0 -> x1, Pallas kernels: none -> 5.15 us  [body(): pl.pallas_call(hand_over, out_shape=outs, in_specs=[anywhere] * 3, out_sp...]
    unnamed x7 -> x0, local copies, waits for them, and re-layouts: 2.73 us -> none
where the time goes in v4:
time: 40.2 us; the launch traced here: 40.1 us
  Pallas kernels  39.4 us (98%)
  between operations  0.64 us (2%)
    pallas_call x1, Pallas kernels, body(): pl.pallas_call(functools.partial(update_kernel, n_src, n_seg, knots, 32),...  34.3 us
    pallas_call x1, Pallas kernels, body(): pl.pallas_call(hand_over, out_shape=outs, in_specs=[anywhere] * 3, out_sp...  5.15 us

profile of v4, /device:TPU:0, one launch (start us, length us, event | category | flops | bytes accessed | tf_op | source)
XLA Modules:
  0.0 40.1 jit_solution(9811391904213341413)
XLA Ops:
  0.6 34.3 %shard_map.121 = (f32[5,2048]{1,0:T(8,128)}, f32[3,64]{1,0:T(4,128)}, f32[1,16384]{1,0:T(1,128)}) custom-call(f32[1,16384]{1,0:T(1,128)} %bitcast.6, f32[1,16384]{1,0:T(1,128)} %bitcast.7, f32[1,16384]{1,0:T(1,128)} %bitcast.8, f32[5,16384]{1,0:T(8,128)} %sp_in.1, f32[3,16384]{1,0:T(4,128)} %ad_in.1, s32[1,16384]{1,0:T(1,128)} %bitcast.9, ...), custom_call_target="tpu_custom_call" | custom-call | tf_op jit(solution)/shard_map/pallas_call | solution.py:582
  34.9 5.1 %shard_map.122 = (f32[5,2048]{1,0:T(8,128)}, f32[3,64]{1,0:T(4,128)}, f32[1,16384]{1,0:T(1,128)}) custom-call(f32[5,2048]{1,0:T(8,128)} %get-tuple-element.9.a, f32[3,64]{1,0:T(4,128)} %get-tuple-element.10.b, f32[1,16384]{1,0:T(1,128)} %get-tuple-element.11.c), custom_call_target="tpu_custom_call" | custom-call | tf_op jit(solution)/shard_map/pallas_call | solution.py:616

commit v5 on v4

--- a/solution.py
+++ b/solution.py
@@ -325,7 +325,7 @@
         acc[...] += contract_lanes(expand(split, source >> LO_BITS, groups), hot)
         return carry
 
-    lax.fori_loop(0, n_src, source_step, 0)
+    lax.fori_loop(0, n_src, source_step, 0, unroll=2)
     for group in range(groups):
         sums[group] = acc[48 * group : 48 * group + 24] + acc[48 * group + 24 : 48 * group + 48]
 
@@ -552,15 +552,10 @@
     lax.fori_loop(0, n_src, res_stored, 0)
 
 
-def hand_over(a, b, c, a_to, b_to, c_to, sem):
-    copies = [
-        pltpu.make_async_copy(x, y, sem.at[number])
-        for number, (x, y) in enumerate([(c, c_to), (a, a_to), (b, b_to)])
-    ]
-    for copy in copies:
-        copy.start()
-    for copy in copies:
-        copy.wait()
+def hand_over(a, b, c, a_to, b_to, c_to):
+    a_to[...] = a[...]
+    b_to[...] = b[...]
+    c_to[...] = c[...]
 
 
 def body(residual, obs_weight, time_frac, src_partials, att_dir, src_prior, att_prior,
@@ -616,9 +611,8 @@
     src_update, att_update, out = pl.pallas_call(
         hand_over,
         out_shape=outs,
-        in_specs=[anywhere] * 3,
-        out_specs=[anywhere] * 3,
-        scratch_shapes=[dma((3,))],
+        in_specs=[vmem] * 3,
+        out_specs=[vmem] * 3,
         compiler_params=pltpu.CompilerParams(vmem_limit_bytes=56 * 2**20),
     )(*made)
     return src_update, att_update, out.reshape(obs)

time: 40.2 us -> 35.7 us (0.89)
  Pallas kernels: 39.4 us -> 34.9 us
    pallas_call x1, Pallas kernels: 5.15 us -> 1.54 us  [body(): pl.pallas_call(hand_over, out_shape=outs, in_specs=[vmem] * 3, out_specs=...]
    pallas_call x1, Pallas kernels: 34.3 us -> 33.4 us  [body(): pl.pallas_call(functools.partial(update_kernel, n_src, n_seg, knots, 32),...]
where the time goes in v5:
time: 35.7 us; the launch traced here: 35.5 us
  Pallas kernels  34.9 us (98%)
  between operations  0.64 us (2%)
    pallas_call x1, Pallas kernels, body(): pl.pallas_call(functools.partial(update_kernel, n_src, n_seg, knots, 32),...  33.4 us
    pallas_call x1, Pallas kernels, body(): pl.pallas_call(hand_over, out_shape=outs, in_specs=[vmem] * 3, out_specs=...  1.54 us

profile of v5, /device:TPU:0, one launch (start us, length us, event | category | flops | bytes accessed | tf_op | source)
XLA Modules:
  0.0 35.5 jit_solution(11581214514009885761)
XLA Ops:
  0.6 33.4 %shard_map.121 = (f32[5,2048]{1,0:T(8,128)}, f32[3,64]{1,0:T(4,128)}, f32[1,16384]{1,0:T(1,128)}) custom-call(f32[1,16384]{1,0:T(1,128)} %bitcast.6, f32[1,16384]{1,0:T(1,128)} %bitcast.7, f32[1,16384]{1,0:T(1,128)} %bitcast.8, f32[5,16384]{1,0:T(8,128)} %sp_in.1, f32[3,16384]{1,0:T(4,128)} %ad_in.1, s32[1,16384]{1,0:T(1,128)} %bitcast.9, ...), custom_call_target="tpu_custom_call" | custom-call | tf_op jit(solution)/shard_map/pallas_call | solution.py:577
  34.0 1.5 %shard_map.122 = (f32[5,2048]{1,0:T(8,128)}, f32[3,64]{1,0:T(4,128)}, f32[1,16384]{1,0:T(1,128)}) custom-call(f32[5,2048]{1,0:T(8,128)} %get-tuple-element.9.a, f32[3,64]{1,0:T(4,128)} %get-tuple-element.10.b, f32[1,16384]{1,0:T(1,128)} %get-tuple-element.11.c), custom_call_target="tpu_custom_call" | custom-call | tf_op jit(solution)/shard_map/pallas_call | solution.py:611

commit v6 on v5

--- a/solution.py
+++ b/solution.py
@@ -325,7 +325,7 @@
         acc[...] += contract_lanes(expand(split, source >> LO_BITS, groups), hot)
         return carry
 
-    lax.fori_loop(0, n_src, source_step, 0, unroll=2)
+    lax.fori_loop(0, n_src, source_step, 0, unroll=4)
     for group in range(groups):
         sums[group] = acc[48 * group : 48 * group + 24] + acc[48 * group + 24 : 48 * group + 48]
 

time: 35.7 us -> 35.3 us (0.989)
  Pallas kernels: 34.9 us -> 34.5 us
    pallas_call x1, Pallas kernels: 33.4 us -> 32.9 us  [body(): pl.pallas_call(functools.partial(update_kernel, n_src, n_seg, knots, 32),...]
where the time goes in v6:
time: 35.3 us; the launch traced here: 35.1 us
  Pallas kernels  34.5 us (98%)
  between operations  0.64 us (2%)
    pallas_call x1, Pallas kernels, body(): pl.pallas_call(functools.partial(update_kernel, n_src, n_seg, knots, 32),...  32.9 us
    pallas_call x1, Pallas kernels, body(): pl.pallas_call(hand_over, out_shape=outs, in_specs=[vmem] * 3, out_specs=...  1.54 us

profile of v6, /device:TPU:0, one launch (start us, length us, event | category | flops | bytes accessed | tf_op | source)
XLA Modules:
  0.0 35.1 jit_solution(204709838740162997)
XLA Ops:
  0.6 32.9 %shard_map.121 = (f32[5,2048]{1,0:T(8,128)}, f32[3,64]{1,0:T(4,128)}, f32[1,16384]{1,0:T(1,128)}) custom-call(f32[1,16384]{1,0:T(1,128)} %bitcast.6, f32[1,16384]{1,0:T(1,128)} %bitcast.7, f32[1,16384]{1,0:T(1,128)} %bitcast.8, f32[5,16384]{1,0:T(8,128)} %sp_in.1, f32[3,16384]{1,0:T(4,128)} %ad_in.1, s32[1,16384]{1,0:T(1,128)} %bitcast.9, ...), custom_call_target="tpu_custom_call" | custom-call | tf_op jit(solution)/shard_map/pallas_call | solution.py:577
  33.6 1.5 %shard_map.122 = (f32[5,2048]{1,0:T(8,128)}, f32[3,64]{1,0:T(4,128)}, f32[1,16384]{1,0:T(1,128)}) custom-call(f32[5,2048]{1,0:T(8,128)} %get-tuple-element.9.a, f32[3,64]{1,0:T(4,128)} %get-tuple-element.10.b, f32[1,16384]{1,0:T(1,128)} %get-tuple-element.11.c), custom_call_target="tpu_custom_call" | custom-call | tf_op jit(solution)/shard_map/pallas_call | solution.py:611
